TPU v7x, 256 devices: a whole 4x4x8 slice. The times are simulated.
256 devices in a mesh: seg: 128 (over y, x, z_lo, core), feat: 2 (over z_hi).
Axes of the slice: x: 4, y: 4, z: 8 (z_hi: 2, z_lo: 4; z = z_hi * 4 + z_lo), core: 2. Of those that a mesh axis runs over, the one named last changes fastest.
Arguments:
- train_feats: bfloat16 [65536, 8192], P('seg', 'feat'), may hold values from -24 to 24
- test_feats: bfloat16 [8192, 8192], P('seg', 'feat'), may hold values from -6 to 6
- factor_panel: bfloat16 [8192, 256], P('feat'), may hold values from -0.0625 to 0.0625
Outputs:
- gram_panel: float32 [256, 8192], P('seg', 'feat')
- scores: bfloat16 [65536, 8192], P(('seg', 'feat'))
All inputs are finite; a program needn't handle non-finite values.
Results may differ from a plain program's by a relative error of at most 0.0057.
Values may be sent and summed in bfloat16 or wider, within the bound.
No kernel may reach another device: no remote copies, remote signals or barrier semaphores. Data moves between devices by JAX's collectives and lax.ppermute only.
A program may use at most 64 MiB of HBM per device.

v0:
```python
import math

import jax
import jax.numpy as jnp
from jax import lax
from jax.sharding import PartitionSpec as P

W = 256


def spread(value, axis, source):
    kept = jnp.where(lax.axis_index(axis) == source, value, 0).astype(value.dtype)
    return lax.psum(kept, axis)


def local(train_feats, test_feats, factor_panel):
    seg_count = lax.axis_size("seg")
    width = W
    n_train = train_feats.shape[0] * seg_count
    panel_cols = spread(train_feats[:, :width], "feat", 0)
    term = lax.dot_general(
        panel_cols, train_feats, (((0,), (0,)), ((), ())), preferred_element_type=jnp.float32
    )
    mine = lax.psum_scatter(term, "seg", scatter_dimension=0, tiled=True)
    gram_panel = mine / n_train
    train_part = jnp.dot(train_feats, factor_panel, preferred_element_type=jnp.float32)
    proj_train = lax.psum_scatter(train_part, "feat", scatter_dimension=0, tiled=True).astype(
        jnp.bfloat16
    )
    test_part = jnp.dot(test_feats, factor_panel, preferred_element_type=jnp.float32)
    scale = 1.0 / math.sqrt(factor_panel.shape[1])
    proj_test = lax.psum(test_part, "feat").astype(jnp.bfloat16)
    block_scores = lax.dot_general(
        proj_train,
        lax.all_gather(proj_test, "seg", axis=0, tiled=True),
        (((1,), (1,)), ((), ())),
        preferred_element_type=jnp.float32,
    )
    scores = (block_scores * scale).astype(jnp.bfloat16)
    return (gram_panel, scores)


def solution(mesh):
    in_specs = (P("seg", "feat"), P("seg", "feat"), P("feat", None))
    out_specs = (P("seg", "feat"), P(("seg", "feat"), None))
    return jax.shard_map(local, mesh=mesh, in_specs=in_specs, out_specs=out_specs, check_vma=False)
```

profile of v0, /device:TPU:1, one launch (start us, length us, event | category | flops | bytes accessed | tf_op | source)
XLA Modules:
  0.0 1614.4 jit_solution(9904591364793209086)
XLA Ops:
  7.2 0.0 copy-start
  7.2 0.0 all-reduce.4.cloned.1.call-start
  7.2 1.8 slice_select_fusion
  9.0 0.0 all-reduce.4.cloned.1.call-update
  9.1 0.0 all-reduce.6.cloned.1.call-start
  9.1 49.7 %all-reduce.4.cloned.1.call-done = bf16[512,256]{1,0:T(8,128)(2,1)} async-done(((bf16[512,256]{1,0:T(8,128)(2,1)}), bf16[512,256]{1,0:T(8,128)(2,1)}) %all-reduce.4.cloned.1.call-update) | async-done | bytes 262160 | tf_op jit(solution)/shard_map/psum | solution.py:13
  58.8 5.6 fusion.2
  64.4 0.0 all-reduce.6.cloned.1.call-update
  64.4 0.0 copy-start.1
  64.4 0.0 copy-start.2
  64.4 0.0 reduce-scatter.2.cloned.1.call-start
  64.5 0.0 copy-done
  64.5 4.3 fusion.3
  68.8 0.0 reduce-scatter.2.cloned.1.call-update
  68.8 0.0 all-gather.2.cloned.1.call-start
  68.9 0.0 copy-done.1
  68.9 0.5 fusion.4
  69.4 11.1 psum.15
  80.5 0.0 all-gather.2.cloned.1.call-update
  80.5 0.0 copy-done.2
  80.5 0.6 dynamic-slice
  81.8 1289.5 %all-reduce.6.cloned.1.call-done = f32[256,4096]{1,0:T(8,128)} async-done(((f32[256,4096]{1,0:T(8,128)}), f32[256,4096]{1,0:T(8,128)}) %all-reduce.6.cloned.1.call-update) | async-done | bytes 4194320
  1371.3 1.5 dynamic-slice_multiply_fusion
  1372.8 30.9 %reduce-scatter.2.cloned.1.call-done = f32[256,256]{1,0:T(8,128)} async-done(((f32[512,256]{1,0:T(8,128)}), f32[256,256]{1,0:T(8,128)}) %reduce-scatter.2.cloned.1.call-update) | async-done | bytes 262160 | tf_op jit(solution)/shard_map/reduce_scatter | solution.py:27
  1403.7 198.6 %all-gather.2.cloned.1.call-done = bf16[8192,256]{1,0:T(8,128)(2,1)} async-done(((bf16[64,256]{1,0:T(8,128)(2,1)}), bf16[8192,256]{1,0:T(8,128)(2,1)}) %all-gather.2.cloned.1.call-update) | async-done | bytes 4194320 | tf_op jit(solution)/shard_map/all_gather | solution.py:35
  1602.3 5.6 fusion
Async XLA Ops:
  7.2 57.3 %copy-start = (bf16[4096,256]{1,0:T(8,128)(2,1)S(1)}, bf16[4096,256]{1,0:T(8,128)(2,1)}, u32[]{:S(2)}) copy-start(bf16[4096,256]{1,0:T(8,128)(2,1)} %param.5) | copy-start | bytes 6291460
  7.2 51.6 %all-reduce.4.cloned.1.call-start = ((), (), s32[]{:S(2)}) async-start(), calls=%async_computation.1 | async-start | bytes 524288 | tf_op jit(solution)/shard_map/psum | solution.py:13
  9.1 1362.2 %all-reduce.6.cloned.1.call-start = ((), (), s32[]{:S(2)}) async-start(), calls=%async_computation.4 | async-start | bytes 8388608
  64.4 4.5 copy-start.1
  64.4 16.1 copy-start.2
  64.4 1339.3 %reduce-scatter.2.cloned.1.call-start = ((), (), s32[]{:S(2)}) async-start(), calls=%async_computation.2 | async-start | bytes 786432 | tf_op jit(solution)/shard_map/reduce_scatter | solution.py:27
  68.8 1533.5 %all-gather.2.cloned.1.call-start = ((), (), s32[]{:S(2)}) async-start(), calls=%async_computation.3 | async-start | bytes 4227072 | tf_op jit(solution)/shard_map/all_gather | solution.py:35
Sparse Core Ops, SparseCore 0:
  11.2 47.5 all-reduce.3
  64.5 1306.7 all-reduce.5
  1373.8 29.8 reduce-scatter.1
  1405.6 196.6 all-gather.1
where the time goes:
time: 1610 us
  waiting for transfers between devices  1570 us (98%)
    unnamed x5, waiting for transfers between devices  1290 us
    all_gather x1, waiting for transfers between devices, local(): lax.all_gather(proj_test, 'seg', axis=0, tiled=True)  199 us
    psum x1, waiting for transfers between devices, spread(): return lax.psum(kept, axis)  49.7 us
  transfers between devices with their start and end apart: 4, of which 4 were waited for; matrix products, arithmetic and copies ran while one was open for 0% of the time, Pallas kernels for 0%

commit v1 on v0

v1 whole, which is shorter than its diff:
```python
import math

import jax
import jax.numpy as jnp
from jax import lax
from jax.experimental import pallas as pl
from jax.experimental.pallas import tpu as pltpu
from jax.sharding import Mesh, PartitionSpec as P

W = 256
AXES = ("y", "x", "l", "c", "h")
SIZES = (4, 4, 4, 2, 2)
VMEM = 48 * 1024 * 1024


def pairs(move, keep=None):
    out = []
    for i in range(math.prod(SIZES)):
        h, c, l, yx = i % 2, i // 2 % 2, i // 4 % 4, i // 16
        if keep is None or keep(l, c, h):
            l2, c2, h2 = move(l, c, h)
            out.append((i, ((yx * 4 + l2) * 2 + c2) * 2 + h2))
    return out


OTHER_HALF = pairs(lambda l, c, h: (l, c, 1 - h))
TO_SECOND_HALF = pairs(lambda l, c, h: (l, c, 1), lambda l, c, h: h == 0)
OTHER_CORE = pairs(lambda l, c, h: (l, 1 - c, h))
ALONG = [pairs(lambda l, c, h, d=d: ((l + d) % 4, c, h)) for d in range(4)]


def pack_kernel(mine_ref, got_ref, proj_ref, out_ref):
    both = mine_ref[...] + got_ref[...].astype(jnp.float32)
    for dest in range(2):
        out_ref[dest, :256, :] = proj_ref[...]
        rows = both[8 * dest : 8 * dest + 8, :]
        for p in range(8):
            two = jnp.concatenate(
                [rows[:, 512 * p : 512 * p + 256], rows[:, 512 * p + 256 : 512 * p + 512]], axis=0
            )
            out_ref[dest, 256 + 16 * p : 272 + 16 * p, :] = two.astype(jnp.bfloat16)


def pack(mine, got, proj):
    return pl.pallas_call(
        pack_kernel,
        grid=(8,),
        in_specs=[
            pl.BlockSpec((16, 4096), lambda i: (i, 0)),
            pl.BlockSpec((16, 4096), lambda i: (i, 0)),
            pl.BlockSpec((256, 256), lambda i: (0, 0)),
        ],
        out_specs=pl.BlockSpec((2, 384, 256), lambda i: (i, 0, 0)),
        out_shape=jax.ShapeDtypeStruct((16, 384, 256), jnp.bfloat16),
        compiler_params=pltpu.CompilerParams(vmem_limit_bytes=VMEM),
        cost_estimate=pl.CostEstimate(flops=524288, bytes_accessed=6 << 20, transcendentals=0),
        name="pack",
    )(mine, got, proj)


def fold_kernel(in_ref, own_ref, a_ref, b_ref, d_ref, sum_ref):
    total = in_ref[0].astype(jnp.float32)
    for s in range(1, 16):
        total = total + in_ref[s].astype(jnp.float32)
    sum_ref[0] = total[:, :128]
    sum_ref[1] = total[:, 128:]
    for step, ref in enumerate((own_ref, a_ref, b_ref, d_ref)):
        for j in range(2):
            for half in range(2):
                rows = sum_ref[half, pl.ds(2 * step + j, 16, stride=8), :]
                ref[16 * j : 16 * j + 16, 128 * half : 128 * half + 128] = rows.astype(ref.dtype)


def fold(merged):
    whole = pl.BlockSpec((32, 256), lambda i: (0, 0))
    return pl.pallas_call(
        fold_kernel,
        grid=(1,),
        in_specs=[pl.BlockSpec((16, 128, 256), lambda i: (0, 2, 0))],
        out_specs=[whole] * 4,
        out_shape=[jax.ShapeDtypeStruct((32, 256), jnp.float32)]
        + [jax.ShapeDtypeStruct((32, 256), jnp.bfloat16)] * 3,
        scratch_shapes=[pltpu.VMEM((2, 128, 128), jnp.float32)],
        compiler_params=pltpu.CompilerParams(vmem_limit_bytes=VMEM),
        cost_estimate=pl.CostEstimate(flops=524288, bytes_accessed=1 << 20, transcendentals=0),
        name="fold",
    )(merged)


def scores_kernel(core_ref, train_ref, own_ref, other_ref, out_ref, both_ref):
    core = core_ref[0]
    for s in range(2):
        for l in range(4):
            base = 512 * s + 128 * l
            mine = pl.multiple_of(base + 64 * core, 64)
            theirs = pl.multiple_of(base + 64 * (1 - core), 64)
            both_ref[pl.ds(mine, 64), :] = own_ref[s, 64 * l : 64 * l + 64, :]
            both_ref[pl.ds(theirs, 64), :] = other_ref[s, 64 * l : 64 * l + 64, :]
    product = lax.dot_general(
        train_ref[...], both_ref[...], (((1,), (1,)), ((), ())), preferred_element_type=jnp.float32
    )
    out_ref[...] = (product * (1.0 / math.sqrt(256))).astype(jnp.bfloat16)


def scores_of(core, proj_train, own, other):
    return pl.pallas_call(
        scores_kernel,
        grid_spec=pltpu.PrefetchScalarGridSpec(
            num_scalar_prefetch=1,
            grid=(8,),
            in_specs=[
                pl.BlockSpec((256, 256), lambda i, c: (0, 0)),
                pl.BlockSpec((2, 256, 256), lambda i, c: (i, 0, 0)),
                pl.BlockSpec((2, 256, 256), lambda i, c: (i, 0, 0)),
            ],
            out_specs=pl.BlockSpec((256, 1024), lambda i, c: (0, i)),
            scratch_shapes=[pltpu.VMEM((1024, 256), jnp.bfloat16)],
        ),
        out_shape=jax.ShapeDtypeStruct((256, 8192), jnp.bfloat16),
        compiler_params=pltpu.CompilerParams(vmem_limit_bytes=VMEM),
        cost_estimate=pl.CostEstimate(flops=1 << 30, bytes_accessed=8 << 20, transcendentals=0),
        name="scores",
    )(core, proj_train, own, other)


def local(train_feats, test_feats, factor_panel):
    f32, bf16 = jnp.float32, jnp.bfloat16
    l, c, h = lax.axis_index("l"), lax.axis_index("c"), lax.axis_index("h")

    first = train_feats[:, :W]
    panel = jnp.where(h == 0, first, lax.ppermute(first, AXES, TO_SECOND_HALF))
    place = jnp.arange(W)
    core_of, yx_of, step_of, j_of = place // 128, place // 8 % 16, place // 2 % 4, place % 2
    column = ((yx_of * 4 + (l + step_of) % 4) * 2 + (c + core_of) % 2) * 2 + j_of
    choose = (jnp.arange(W)[:, None] == column[None, :]).astype(bf16)
    ordered = jnp.dot(panel, choose, preferred_element_type=f32).astype(bf16)
    term = lax.dot_general(ordered, train_feats, (((0,), (0,)), ((), ())), preferred_element_type=f32)
    got = lax.ppermute(term[128:].astype(bf16), AXES, OTHER_CORE)

    part = jnp.dot(test_feats, factor_panel, preferred_element_type=f32).astype(bf16)
    parts = lax.all_to_all(jnp.broadcast_to(part, (8, 64, 256)), ("h", "l"), 0, 0, tiled=True)
    parts = parts.reshape(2, 256, 256).astype(f32)
    proj_test = (parts[0] + parts[1]).astype(bf16)

    merged = lax.all_to_all(pack(term[:128], got, proj_test), ("y", "x"), 0, 0, tiled=True)

    own, *sent = fold(merged)
    total = own
    for d, block in enumerate(sent, 1):
        total = total + lax.ppermute(block, AXES, ALONG[d]).astype(f32)
    gram_panel = total.reshape(2, 4096) / 65536

    train_part = jnp.dot(train_feats, factor_panel, preferred_element_type=f32)
    keep = lax.dynamic_slice_in_dim(train_part, h * 256, 256)
    give = lax.dynamic_slice_in_dim(train_part, (1 - h) * 256, 256)
    proj_train = (keep + lax.ppermute(give, AXES, OTHER_HALF)).astype(bf16)
    gathered = merged[:, :256, :]
    other = lax.ppermute(gathered, AXES, OTHER_CORE)
    scores = scores_of(c.astype(jnp.int32)[None], proj_train, gathered, other)
    return (gram_panel, scores)


def solution(mesh):
    fine = Mesh(mesh.devices.reshape(SIZES), AXES)
    seg = ("y", "x", "l", "c")
    in_specs = (P(seg, "h"), P(seg, "h"), P("h", None))
    out_specs = (P(seg, "h"), P((*seg, "h"), None))
    return jax.shard_map(local, mesh=fine, in_specs=in_specs, out_specs=out_specs, check_vma=False)
```

time: 1610 us -> 139 us (0.09)
  waiting for transfers between devices: 1570 us -> 25 us
  blocking collectives: 11.1 us -> 45.5 us
  starting transfers between devices: 0.16 us -> 30 us
    unnamed x5 -> x0, waiting for transfers between devices: 1290 us -> none
    all_gather x1 -> x0, waiting for transfers between devices: 199 us -> none  [local(): lax.all_gather(proj_test, 'seg', axis=0, tiled=True)]
    psum x1 -> x0, waiting for transfers between devices: 49.7 us -> none  [spread(): return lax.psum(kept, axis)]
    all_to_all x0 -> x1, blocking collectives: none -> 45.5 us  [local(): lax.all_to_all(pack(term[:128], got, proj_test), ('y', 'x'), 0, 0, tiled=...]
    reduce_scatter x1 -> x0, waiting for transfers between devices: 30.9 us -> none  [local(): lax.psum_scatter(train_part, 'feat', scatter_dimension=0, tiled=True)]
    ppermute x0 -> x7, starting transfers between devices: none -> 17.4 us  [the longest x1 9.66 us: local(): panel = jnp.where(h == 0, first, lax.ppermute(first, AXES, TO_SECOND_HALF))]
  transfers between devices with their start and end apart: 4 -> 8, of which waited for: 4 -> 3; matrix products, arithmetic and copies ran while one was open for 0% -> 7% of each run, Pallas kernels for 0% -> 0%
where the time goes in v1:
time: 139 us; the launch traced here: 138 us
  blocking collectives  45.5 us (33%)
  starting transfers between devices  30 us (22%)
  waiting for transfers between devices  25 us (18%)
  local copies, waits for them, and re-layouts  14.9 us (11%)
  Pallas kernels  11.1 us (8%)
  matrix products  10.8 us (8%)
    all_to_all x1, blocking collectives, local(): lax.all_to_all(pack(term[:128], got, proj_test), ('y', 'x'), 0, 0, tiled=...  45.5 us
    all_to_all x1, starting transfers between devices, local(): lax.all_to_all(jnp.broadcast_to(part, (8, 64, 256)), ('h', 'l'), 0, 0, ti...  12.6 us
    ppermute x1, waiting for transfers between devices, local(): proj_train = (keep + lax.ppermute(give, AXES, OTHER_HALF)).astype(bf16)  10.8 us
    ppermute x1, starting transfers between devices, local(): panel = jnp.where(h == 0, first, lax.ppermute(first, AXES, TO_SECOND_HALF))  9.66 us
    all_to_all x1, waiting for transfers between devices, local(): lax.all_to_all(jnp.broadcast_to(part, (8, 64, 256)), ('h', 'l'), 0, 0, ti...  9.25 us
    pallas_call x1, Pallas kernels, scores_of(): pl.pallas_call(scores_kernel, grid_spec=pltpu.PrefetchScalarGridSpec(num_...  7.7 us
    dot_general x1, matrix products, local(): lax.dot_general(ordered, train_feats, (((0,), (0,)), ((), ())), preferred...  5.86 us
    unnamed x8, local copies, waits for them, and re-layouts  5.14 us
  transfers between devices with their start and end apart: 8, of which 3 were waited for; matrix products, arithmetic and copies ran while one was open for 7% of the time, Pallas kernels for 0%

profile of v1, /device:TPU:1, one launch (start us, length us, event | category | flops | bytes accessed | tf_op | source)
XLA Modules:
  0.0 138.2 jit_solution(11240207633156031382)
XLA Ops:
  0.6 0.0 copy-start
  0.6 1.1 slice.21
  1.8 9.7 %collective-permute-start = (bf16[512,256]{1,0:T(8,128)(2,1)S(1)}, bf16[512,256]{1,0:T(8,128)(2,1)S(1)}, u32[]{:S(2)}, u32[]{:S(2)}) collective-permute-start(bf16[512,256]{1,0:T(8,128)(2,1)S(1)} %slice.21), channel_id=1, source_target_pairs={{0,1},{2,3},{4,5},{6,7},{8,9},{10,11},{12,13},{14,15},{16,17},{18,... | collective-permute-start | bytes 786440 | tf_op jit(solution)/shard_map/ppermute | solution.py:131
  11.5 4.9 %collective-permute-done = bf16[512,256]{1,0:T(8,128)(2,1)S(1)} collective-permute-done((bf16[512,256]{1,0:T(8,128)(2,1)S(1)}, bf16[512,256]{1,0:T(8,128)(2,1)S(1)}, u32[]{:S(2)}, u32[]{:S(2)}) %collective-permute-start) | collective-permute-done | bytes 262176 | tf_op jit(solution)/shard_map/ppermute | solution.py:131
  16.4 5.9 %fusion = f32[256,4096]{1,0:T(8,128)} fusion(bf16[512,4096]{1,0:T(8,128)(2,1)} %param.3, bf16[512,256]{1,0:T(8,128)(2,1)S(1)} %collective-permute-done, pred[]{:T(512)S(6)} %eq.22, s32[256]{0:T(256)S(1)} %fusion.9), kind=kOutput, calls=%fused_computation.2 | convolution fusion | flops 1141178368 | bytes 8913921 | tf_op jit(solution)/shard_map/dot_general | solution.py:137
  22.2 2.7 %slice.42 = bf16[128,4096]{1,0:T(8,128)(2,1)} slice(f32[256,4096]{1,0:T(8,128)} %fusion), slice={[128:256], [0:4096]} | slice | bytes 2097152 | tf_op jit(solution)/shard_map/slice | solution.py:138
  24.9 1.5 %collective-permute-start.1 = (bf16[128,4096]{1,0:T(8,128)(2,1)}, bf16[128,4096]{1,0:T(8,128)(2,1)S(1)}, u32[]{:S(2)}, u32[]{:S(2)}) collective-permute-start(bf16[128,4096]{1,0:T(8,128)(2,1)} %slice.42), channel_id=1, source_target_pairs={{0,2},{1,3},{2,0},{3,1},{4,6},{5,7},{6,4},{7,5},{8,10},{9,11},{10,... | collective-permute-start | bytes 3145736 | tf_op jit(solution)/shard_map/ppermute | solution.py:138
  26.5 1.5 %convolution_convert_fusion.1 = bf16[64,256]{1,0:T(8,128)(2,1)S(1)} fusion(bf16[64,4096]{1,0:T(8,128)(2,1)} %param.4, bf16[4096,256]{1,0:T(8,128)(2,1)S(1)} %copy-done), kind=kOutput, calls=%fused_computation.3 | convolution fusion | flops 134234112 | bytes 2654208 | tf_op jit(solution)/shard_map/dot_general | solution.py:140
  28.0 0.7 broadcast_in_dim.8
  28.7 12.6 %all-to-all-start = ((bf16[8,64,256]{2,1,0:T(8,128)(2,1)}), bf16[8,64,256]{2,1,0:T(8,128)(2,1)S(1)}, u32[]{:S(2)}, u32[]{:S(2)}) async-start(bf16[8,64,256]{2,1,0:T(8,128)(2,1)} %broadcast_in_dim.8), calls=%async_computation | async-start | bytes 524288 | tf_op jit(solution)/shard_map/all_to_all | solution.py:141
  41.3 3.1 %slice.27.mine_ref = f32[128,4096]{1,0:T(8,128)} slice(f32[256,4096]{1,0:T(8,128)} %fusion), slice={[0:128], [0:4096]} | slice | bytes 4194304 | tf_op jit(solution)/shard_map/slice | solution.py:145
  44.4 9.2 %all-to-all-done = bf16[8,64,256]{2,1,0:T(8,128)(2,1)S(1)} async-done(((bf16[8,64,256]{2,1,0:T(8,128)(2,1)}), bf16[8,64,256]{2,1,0:T(8,128)(2,1)S(1)}, u32[]{:S(2)}, u32[]{:S(2)}) %all-to-all-start) | async-done | bytes 262176 | tf_op jit(solution)/shard_map/all_to_all | solution.py:141
  53.7 0.0 collective-permute-done.1.got_ref
  53.7 1.6 %copy-done.3 = f32[128,4096]{1,0:T(8,128)S(1)} copy-done((f32[128,4096]{1,0:T(8,128)S(1)}, f32[128,4096]{1,0:T(8,128)}, u32[]{:S(2)}) %copy-start.3) | copy-done | bytes 2097176
  55.3 3.2 %pack.1 = bf16[16,384,256]{2,1,0:T(8,128)(2,1)} custom-call(f32[128,4096]{1,0:T(8,128)S(1)} %copy-done.3, bf16[128,4096]{1,0:T(8,128)(2,1)S(1)} %collective-permute-done.1.got_ref, bf16[256,256]{1,0:T(8,128)(2,1)S(1)} %bitcast.7), custom_call_target="tpu_custom_call" | custom-call | flops 524288 | bytes 6291456 | tf_op jit(solution)/shard_map/pack/pallas_call | solution.py:45
  58.6 45.5 %all_to_all.10.in_ref = bf16[16,384,256]{2,1,0:T(8,128)(2,1)S(1)} all-to-all(bf16[16,384,256]{2,1,0:T(8,128)(2,1)} %pack.1), channel_id=1, replica_groups=mesh['y'=4,'x'=4,'l'=4,'c'=2,'h'=2] {'y','x'}, dimensions={0} | all-to-all | bytes 6291456 | tf_op jit(solution)/shard_map/all_to_all | solution.py:145
  104.0 1.5 %slice.31.own_ref = bf16[16,256,256]{2,1,0:T(8,128)(2,1)} slice(bf16[16,384,256]{2,1,0:T(8,128)(2,1)S(1)} %all_to_all.10.in_ref), slice={[0:16], [0:256], [0:256]} | slice | bytes 4194304 | tf_op jit(solution)/shard_map/slice | solution.py:157
  105.5 1.7 %copy-done.1 = bf16[16,384,256]{2,1,0:T(8,128)(2,1)} copy-done((bf16[16,384,256]{2,1,0:T(8,128)(2,1)}, bf16[16,384,256]{2,1,0:T(8,128)(2,1)S(1)}, u32[]{:S(2)}) %copy-start.1) | copy-done | bytes 3145752
  107.1 1.9 %collective-permute-start.6 = (bf16[16,256,256]{2,1,0:T(8,128)(2,1)}, bf16[16,256,256]{2,1,0:T(8,128)(2,1)}, u32[]{:S(2)}, u32[]{:S(2)}) collective-permute-start(bf16[16,256,256]{2,1,0:T(8,128)(2,1)} %slice.31.own_ref), channel_id=1, source_target_pairs={{0,2},{1,3},{2,0},{3,1},{4,6},{5,7},{6,4},{7,5},{8,10},{9,11},{10,... | collective-permute-start | bytes 6291464 | tf_op jit(solution)/shard_map/ppermute | solution.py:158
  109.0 3.4 %fusion.24 = f32[512,256]{1,0:T(8,128)S(1)} fusion(bf16[512,4096]{1,0:T(8,128)(2,1)} %param.3, bf16[4096,256]{1,0:T(8,128)(2,1)S(1)} %copy-done), kind=kOutput, calls=%fused_computation.51 | convolution fusion | flops 1073741824 | bytes 6815744 | tf_op jit(solution)/shard_map/dot_general | solution.py:153
  112.5 0.1 collective-permute-start.5
  112.6 0.0 copy-start.2
  112.6 1.9 %copy-done.2 = bf16[16,384,256]{2,1,0:T(8,128)(2,1)S(1)} copy-done((bf16[16,384,256]{2,1,0:T(8,128)(2,1)S(1)}, bf16[16,384,256]{2,1,0:T(8,128)(2,1)}, u32[]{:S(2)}) %copy-start.2) | copy-done | bytes 3145752
  114.5 0.2 fold.1
  114.7 1.0 collective-permute-start.2
  115.7 1.0 collective-permute-start.3
  116.7 2.3 %collective-permute-start.4 = (bf16[32,256]{1,0:T(8,128)(2,1)S(1)}, bf16[32,256]{1,0:T(8,128)(2,1)S(1)}, u32[]{:S(2)}, u32[]{:S(2)}) collective-permute-start(bf16[32,256]{1,0:T(8,128)(2,1)S(1)} %get-tuple-element.9), channel_id=1, source_target_pairs={{0,12},{1,13},{2,14},{3,15},{4,0},{5,1},{6,2},{7,3},{8,4},{9,5},{1... | collective-permute-start | bytes 49160 | tf_op jit(solution)/shard_map/ppermute | solution.py:150
  118.9 10.8 %collective-permute-done.5 = f32[256,256]{1,0:T(8,128)S(1)} collective-permute-done((f32[256,256]{1,0:T(8,128)S(1)}, f32[256,256]{1,0:T(8,128)S(1)}, u32[]{:S(2)}, u32[]{:S(2)}) %collective-permute-start.5) | collective-permute-done | bytes 262176 | tf_op jit(solution)/shard_map/ppermute | solution.py:156
  129.8 0.0 collective-permute-done.2
  129.8 0.0 collective-permute-done.3
  129.8 0.6 div.30
  130.5 7.7 %scores.1 = bf16[256,8192]{1,0:T(8,128)(2,1)} custom-call(s32[1]{0:T(128)} %bitcast.1.core_ref, bf16[256,256]{1,0:T(8,128)(2,1)S(1)} %add_convert_fusion.train_ref, bf16[16,256,256]{2,1,0:T(8,128)(2,1)} %slice.31.own_ref, bf16[16,256,256]{2,1,0:T(8,128)(2,1)} %collective-permute-done.6.other_ref), custom_call_target="tpu_custom_call" | custom-call | flops 1073741824 | bytes 8388608 | tf_op jit(solution)/shard_map/scores/pallas_call | solution.py:106
  (11 shorter events, 0.2 us)
Async XLA Ops:
  0.6 25.8 %copy-start = (bf16[4096,256]{1,0:T(8,128)(2,1)S(1)}, bf16[4096,256]{1,0:T(8,128)(2,1)}, u32[]{:S(2)}) copy-start(bf16[4096,256]{1,0:T(8,128)(2,1)} %param.5) | copy-start | bytes 6291460
  1.8 14.6 %collective-permute-start = (bf16[512,256]{1,0:T(8,128)(2,1)S(1)}, bf16[512,256]{1,0:T(8,128)(2,1)S(1)}, u32[]{:S(2)}, u32[]{:S(2)}) collective-permute-start(bf16[512,256]{1,0:T(8,128)(2,1)S(1)} %slice.21), channel_id=1, source_target_pairs={{0,1},{2,3},{4,5},{6,7},{8,9},{10,11},{12,13},{14,15},{16,17},{18,... | collective-permute-start | bytes 786440 | tf_op jit(solution)/shard_map/ppermute | solution.py:131
  24.9 28.8 %collective-permute-start.1 = (bf16[128,4096]{1,0:T(8,128)(2,1)}, bf16[128,4096]{1,0:T(8,128)(2,1)S(1)}, u32[]{:S(2)}, u32[]{:S(2)}) collective-permute-start(bf16[128,4096]{1,0:T(8,128)(2,1)} %slice.42), channel_id=1, source_target_pairs={{0,2},{1,3},{2,0},{3,1},{4,6},{5,7},{6,4},{7,5},{8,10},{9,11},{10,... | collective-permute-start | bytes 3145736 | tf_op jit(solution)/shard_map/ppermute | solution.py:138
  28.7 24.9 %all-to-all-start = ((bf16[8,64,256]{2,1,0:T(8,128)(2,1)}), bf16[8,64,256]{2,1,0:T(8,128)(2,1)S(1)}, u32[]{:S(2)}, u32[]{:S(2)}) async-start(bf16[8,64,256]{2,1,0:T(8,128)(2,1)} %broadcast_in_dim.8), calls=%async_computation | async-start | bytes 524288 | tf_op jit(solution)/shard_map/all_to_all | solution.py:141
  53.7 1.6 %copy-start.3 = (f32[128,4096]{1,0:T(8,128)S(1)}, f32[128,4096]{1,0:T(8,128)}, u32[]{:S(2)}) copy-start(f32[128,4096]{1,0:T(8,128)} %slice.27.mine_ref) | copy-start | bytes 6291460
  105.5 1.7 %copy-start.1 = (bf16[16,384,256]{2,1,0:T(8,128)(2,1)}, bf16[16,384,256]{2,1,0:T(8,128)(2,1)S(1)}, u32[]{:S(2)}) copy-start(bf16[16,384,256]{2,1,0:T(8,128)(2,1)S(1)} %all_to_all.10.in_ref) | copy-start | bytes 9437188
  107.1 23.3 %collective-permute-start.6 = (bf16[16,256,256]{2,1,0:T(8,128)(2,1)}, bf16[16,256,256]{2,1,0:T(8,128)(2,1)}, u32[]{:S(2)}, u32[]{:S(2)}) collective-permute-start(bf16[16,256,256]{2,1,0:T(8,128)(2,1)} %slice.31.own_ref), channel_id=1, source_target_pairs={{0,2},{1,3},{2,0},{3,1},{4,6},{5,7},{6,4},{7,5},{8,10},{9,11},{10,... | collective-permute-start | bytes 6291464 | tf_op jit(solution)/shard_map/ppermute | solution.py:158
  112.5 17.2 %collective-permute-start.5 = (f32[256,256]{1,0:T(8,128)S(1)}, f32[256,256]{1,0:T(8,128)S(1)}, u32[]{:S(2)}, u32[]{:S(2)}) collective-permute-start(f32[256,256]{1,0:T(8,128)S(1)} %constant_dynamic-slice_fusion), channel_id=1, source_target_pairs={{0,1},{1,0},{2,3},{3,2},{4,5},{5,4},{6,7},{7,6},{8,9},{9,8},{10,11... | collective-permute-start | bytes 786440 | tf_op jit(solution)/shard_map/ppermute | solution.py:156
  112.6 1.9 %copy-start.2 = (bf16[16,384,256]{2,1,0:T(8,128)(2,1)S(1)}, bf16[16,384,256]{2,1,0:T(8,128)(2,1)}, u32[]{:S(2)}) copy-start(bf16[16,384,256]{2,1,0:T(8,128)(2,1)} %copy-done.1) | copy-start | bytes 9437188
  114.7 15.1 %collective-permute-start.2 = (bf16[32,256]{1,0:T(8,128)(2,1)S(1)}, bf16[32,256]{1,0:T(8,128)(2,1)S(1)}, u32[]{:S(2)}, u32[]{:S(2)}) collective-permute-start(bf16[32,256]{1,0:T(8,128)(2,1)S(1)} %get-tuple-element.7), channel_id=1, source_target_pairs={{0,4},{1,5},{2,6},{3,7},{4,8},{5,9},{6,10},{7,11},{8,12},{9,13},{1... | collective-permute-start | bytes 49160 | tf_op jit(solution)/shard_map/ppermute | solution.py:150
  115.7 14.1 %collective-permute-start.3 = (bf16[32,256]{1,0:T(8,128)(2,1)S(1)}, bf16[32,256]{1,0:T(8,128)(2,1)S(1)}, u32[]{:S(2)}, u32[]{:S(2)}) collective-permute-start(bf16[32,256]{1,0:T(8,128)(2,1)S(1)} %get-tuple-element.8), channel_id=1, source_target_pairs={{0,8},{1,9},{2,10},{3,11},{4,12},{5,13},{6,14},{7,15},{8,0},{9,1},... | collective-permute-start | bytes 49160 | tf_op jit(solution)/shard_map/ppermute | solution.py:150
  116.7 13.1 %collective-permute-start.4 = (bf16[32,256]{1,0:T(8,128)(2,1)S(1)}, bf16[32,256]{1,0:T(8,128)(2,1)S(1)}, u32[]{:S(2)}, u32[]{:S(2)}) collective-permute-start(bf16[32,256]{1,0:T(8,128)(2,1)S(1)} %get-tuple-element.9), channel_id=1, source_target_pairs={{0,12},{1,13},{2,14},{3,15},{4,0},{5,1},{6,2},{7,3},{8,4},{9,5},{1... | collective-permute-start | bytes 49160 | tf_op jit(solution)/shard_map/ppermute | solution.py:150

commit v2 on v0

v2 whole, which is shorter than its diff:
```python
import math

import jax
import jax.numpy as jnp
from jax import lax
from jax.experimental import pallas as pl
from jax.experimental.pallas import tpu as pltpu
from jax.sharding import Mesh, PartitionSpec as P

W = 256
AXES = ("y", "x", "l", "c", "h")
SIZES = (4, 4, 4, 2, 2)
MIB = 1 << 20
BIG = 56
BF16, F32 = jnp.bfloat16, jnp.float32


def pairs(move, keep=None):
    out = []
    for i in range(math.prod(SIZES)):
        h, c, l, yx = i % 2, i // 2 % 2, i // 4 % 4, i // 16
        if keep is None or keep(l, c, h):
            l2, c2, h2 = move(l, c, h)
            out.append((i, ((yx * 4 + l2) * 2 + c2) * 2 + h2))
    return out


OTHER_HALF = pairs(lambda l, c, h: (l, c, 1 - h))
TO_SECOND_HALF = pairs(lambda l, c, h: (l, c, 1), lambda l, c, h: h == 0)
OTHER_CORE = pairs(lambda l, c, h: (l, 1 - c, h))
ALONG = [pairs(lambda l, c, h, d=d: ((l + d) % 4, c, h)) for d in range(4)]


def params(mib):
    return pltpu.CompilerParams(vmem_limit_bytes=mib * MIB)


def cost(flops, nbytes):
    return pl.CostEstimate(flops=flops, bytes_accessed=nbytes, transcendentals=0)


def anywhere():
    return pl.BlockSpec(memory_space=pltpu.HBM)


def whole():
    return pl.BlockSpec(memory_space=pltpu.VMEM)


def test_kernel(test_ref, factor_ref, after_ref, out_ref, held_ref, test_vmem, sem):
    del after_ref
    copies = []
    for k in range(4):
        part = pl.ds(1024 * k, 1024)
        copies.append(pltpu.make_async_copy(factor_ref.at[part, :], held_ref.at[part, :], sem.at[2 * k]))
        copies.append(
            pltpu.make_async_copy(test_ref.at[:, part], test_vmem.at[:, part], sem.at[2 * k + 1])
        )
    for copy in copies:
        copy.start()
    total = jnp.zeros((64, 256), F32)
    for k in range(4):
        copies[2 * k].wait()
        copies[2 * k + 1].wait()
        total += jnp.dot(
            test_vmem[:, 1024 * k : 1024 * k + 1024],
            held_ref[1024 * k : 1024 * k + 1024, :],
            preferred_element_type=F32,
        )
    part = total.astype(BF16)
    for dest in range(16):
        out_ref[dest] = part[:, 128 * (dest % 2) : 128 * (dest % 2) + 128]


def test_parts(test_feats, factor_panel, after):
    return pl.pallas_call(
        test_kernel,
        in_specs=[anywhere()] * 3,
        out_specs=[whole()] * 2,
        out_shape=[
            jax.ShapeDtypeStruct((16, 64, 128), BF16),
            jax.ShapeDtypeStruct((4096, 256), BF16),
        ],
        scratch_shapes=[pltpu.VMEM((64, 4096), BF16), pltpu.SemaphoreType.DMA((8,))],
        compiler_params=params(8),
        cost_estimate=cost(2 * 64 * 4096 * 256, 5 * MIB),
        name="test_parts",
    )(test_feats, factor_panel, after)


def gram_kernel(at_ref, got_ref, train_ref, mine_ref, theirs_ref):
    l, c, h = at_ref[0], at_ref[1], at_ref[2]
    place = lax.broadcasted_iota(jnp.int32, (256, 256), 0)
    column = lax.broadcasted_iota(jnp.int32, (256, 256), 1)
    yx, l_of, c_of = (place >> 1) & 15, (l + (place >> 5)) & 3, (c + (place >> 7)) & 1
    wanted = (yx << 4) + (l_of << 2) + (c_of << 1) + (place & 1)
    choose = jnp.where(wanted == column, 1.0, 0.0).astype(BF16)
    panel = jnp.where(h == 0, train_ref[:, :W].astype(F32), got_ref[...].astype(F32)).astype(BF16)
    panel = lax.dot_general(choose, panel, (((1,), (1,)), ((), ())), preferred_element_type=F32)
    panel = panel.astype(BF16)
    for i in range(8):
        term = jnp.dot(panel, train_ref[:, 512 * i : 512 * i + 512], preferred_element_type=F32)
        blocks = [term[:, 128 * t : 128 * t + 128].reshape(32, 8, 128) for t in range(4)]
        term = jnp.concatenate(blocks, axis=1)
        mine_ref[:, 32 * i : 32 * i + 32, :] = term[:16]
        theirs_ref[:, 32 * i : 32 * i + 32, :] = term[16:].astype(BF16)


def gram_terms(at, got, train_feats):
    return pl.pallas_call(
        gram_kernel,
        in_specs=[pl.BlockSpec(memory_space=pltpu.SMEM), whole(), whole()],
        out_specs=[whole()] * 2,
        out_shape=[
            jax.ShapeDtypeStruct((16, 256, 128), F32),
            jax.ShapeDtypeStruct((16, 256, 128), BF16),
        ],
        compiler_params=params(16),
        cost_estimate=cost(2 * 256 * 512 * 4096, 7 * MIB),
        name="gram_terms",
    )(at, got, train_feats)


def spread_kernel(parts_ref, out_ref, proj_ref):
    @pl.when(pl.program_id(0) == 0)
    def _():
        proj = (parts_ref[:8].astype(F32) + parts_ref[8:].astype(F32)).reshape(4, 128, 128)
        for l in range(4):
            proj_ref[128 * l : 128 * l + 128, :] = proj[l].T.astype(BF16)

    for dest in range(4):
        out_ref[dest] = proj_ref[...]


def spread(parts):
    return pl.pallas_call(
        spread_kernel,
        grid=(4,),
        in_specs=[pl.BlockSpec((16, 64, 128), lambda i: (0, 0, 0))],
        out_specs=pl.BlockSpec((4, 512, 128), lambda i: (i, 0, 0)),
        out_shape=jax.ShapeDtypeStruct((16, 512, 128), BF16),
        scratch_shapes=[pltpu.VMEM((512, 128), BF16)],
        compiler_params=params(BIG),
        cost_estimate=cost(MIB, 2 * MIB),
        name="spread",
    )(parts)


def cores_kernel(mine_ref, got_ref, own_ref, a_ref, b_ref, d_ref):
    own_ref[...] = mine_ref[:4] + got_ref[:4].astype(F32)
    for step, ref in enumerate((a_ref, b_ref, d_ref), 1):
        rows = slice(4 * step, 4 * step + 4)
        ref[...] = (mine_ref[rows] + got_ref[rows].astype(F32)).astype(BF16)


def sum_cores(mine, got):
    return pl.pallas_call(
        cores_kernel,
        in_specs=[whole()] * 2,
        out_specs=[whole()] * 4,
        out_shape=[jax.ShapeDtypeStruct((4, 256, 128), F32)]
        + [jax.ShapeDtypeStruct((4, 256, 128), BF16)] * 3,
        compiler_params=params(8),
        cost_estimate=cost(MIB // 2, 4 * MIB),
        name="sum_cores",
    )(mine, got)


def line_kernel(own_ref, a_ref, b_ref, d_ref, out_ref, sum_ref):
    sum_ref[...] = own_ref[...] + a_ref[...].astype(F32) + b_ref[...].astype(F32) + d_ref[...].astype(F32)
    for yx in range(16):
        for j in range(2):
            rows = sum_ref[yx // 4, pl.ds(2 * (yx % 4) + j, 32, stride=8), :]
            out_ref[yx, 32 * j : 32 * j + 32, :] = rows.astype(BF16)


def sum_line(own, sums):
    return pl.pallas_call(
        line_kernel,
        in_specs=[whole()] * 4,
        out_specs=whole(),
        out_shape=jax.ShapeDtypeStruct((16, 64, 128), BF16),
        scratch_shapes=[pltpu.VMEM((4, 256, 128), F32)],
        compiler_params=params(8),
        cost_estimate=cost(MIB // 2, 2 * MIB),
        name="sum_line",
    )(own, *sums)


def plane_kernel(in_ref, out_ref):
    total = in_ref[0].astype(F32)
    for s in range(1, 16):
        total = total + in_ref[s].astype(F32)
    out_ref[...] = total / 65536


def sum_plane(rows):
    return pl.pallas_call(
        plane_kernel,
        in_specs=[whole()],
        out_specs=whole(),
        out_shape=jax.ShapeDtypeStruct((64, 128), F32),
        compiler_params=params(8),
        cost_estimate=cost(MIB // 8, MIB // 4),
        name="sum_plane",
    )(rows)


def train_kernel(at_ref, train_ref, factor_ref, keep_ref, give_ref, held_ref, sum_ref, sem):
    copies = []
    for k in range(8):
        part = pl.ds(512 * k, 512)
        copies.append(pltpu.make_async_copy(train_ref.at[:, part], held_ref.at[:, part], sem.at[k]))
    for copy in copies:
        copy.start()
    sum_ref[...] = jnp.zeros_like(sum_ref)
    for k in range(4):
        copies[2 * k].wait()
        copies[2 * k + 1].wait()
        part = slice(1024 * k, 1024 * k + 1024)
        sum_ref[...] += jnp.dot(held_ref[:, part], factor_ref[part, :], preferred_element_type=F32)
    h = at_ref[2]
    keep_ref[...] = sum_ref[pl.ds(pl.multiple_of(256 * h, 256), 256), :]
    give_ref[...] = sum_ref[pl.ds(pl.multiple_of(256 - 256 * h, 256), 256), :].astype(BF16)


def train_parts(at, train_feats, factor_panel):
    return pl.pallas_call(
        train_kernel,
        in_specs=[pl.BlockSpec(memory_space=pltpu.SMEM), anywhere(), whole()],
        out_specs=[whole()] * 3,
        out_shape=[
            jax.ShapeDtypeStruct((256, 256), F32),
            jax.ShapeDtypeStruct((256, 256), BF16),
            jax.ShapeDtypeStruct((512, 4096), BF16),
        ],
        scratch_shapes=[pltpu.VMEM((512, 256), F32), pltpu.SemaphoreType.DMA((8,))],
        compiler_params=params(12),
        cost_estimate=cost(2 * 512 * 4096 * 256, 9 * MIB),
        name="train_parts",
    )(at, train_feats, factor_panel)


def scores_kernel(at_ref, keep_ref, got_ref, own_ref, other_ref, out_ref, proj_ref):
    i = pl.program_id(0)

    @pl.when(i == 0)
    def _():
        c = at_ref[1]
        proj = keep_ref[...] + got_ref[...].astype(F32)
        low, high = proj[:, :128], proj[:, 128:]
        proj_ref[:, :128] = jnp.where(c == 0, low, high).astype(BF16)
        proj_ref[:, 128:] = jnp.where(c == 0, high, low).astype(BF16)

    for n in range(4):
        at = 2 * i + n // 2
        tests = jnp.concatenate(
            [
                jnp.concatenate(
                    [ref[at, 256 * (n % 2) + 128 * t : 256 * (n % 2) + 128 * t + 128, :] for t in range(2)],
                    axis=1,
                )
                for ref in (own_ref, other_ref)
            ],
            axis=0,
        )
        product = jnp.dot(proj_ref[...], tests, preferred_element_type=F32)
        out_ref[:, 256 * n : 256 * n + 256] = (product * (1.0 / math.sqrt(256))).astype(BF16)


def scores_of(at, keep, got, own, other):
    return pl.pallas_call(
        scores_kernel,
        grid=(8,),
        in_specs=[pl.BlockSpec(memory_space=pltpu.SMEM)] + [whole()] * 4,
        out_specs=pl.BlockSpec((256, 1024), lambda i: (0, i)),
        out_shape=jax.ShapeDtypeStruct((256, 8192), BF16),
        scratch_shapes=[pltpu.VMEM((256, 256), BF16)],
        compiler_params=params(12),
        cost_estimate=cost(1 << 30, 8 * MIB),
        name="scores",
    )(at, keep, got, own, other)


def local(train_feats, test_feats, factor_panel):
    at = jnp.stack([lax.axis_index(a) for a in ("l", "c", "h")]).astype(jnp.int32)

    first = train_feats[:, :W]
    sent = lax.ppermute(first, AXES, TO_SECOND_HALF)
    part, factor = test_parts(test_feats, factor_panel, first)
    parts = lax.all_to_all(part, ("h", "l", "c"), 0, 0, tiled=True)
    keep, give, train = train_parts(at, train_feats, factor)
    parts, sent, give = lax.optimization_barrier((parts, sent, give))
    got = lax.ppermute(give, AXES, OTHER_HALF)
    tests = spread(parts)

    sent, _ = lax.optimization_barrier((sent, tests))
    mine, theirs = gram_terms(at, sent, train)
    own, *sums = sum_cores(mine, lax.ppermute(theirs, AXES, OTHER_CORE))
    sums = [lax.ppermute(rows, AXES, ALONG[d]) for d, rows in enumerate(sums, 1)]
    rows = sum_line(own, sums)
    tests = lax.all_to_all(tests, ("y", "x"), 0, 0, tiled=True)
    tests, rows, got = lax.optimization_barrier((tests, rows, got))

    other = lax.ppermute(tests, AXES, OTHER_CORE)
    rows = lax.all_to_all(rows, ("y", "x"), 0, 0, tiled=True)
    scores = scores_of(at, keep, got, tests, other)
    rows, scores = lax.optimization_barrier((rows, scores))
    gram_panel = sum_plane(rows).reshape(2, 4096)
    return (gram_panel, scores)


def solution(mesh):
    fine = Mesh(mesh.devices.reshape(SIZES), AXES)
    seg = ("y", "x", "l", "c")
    in_specs = (P(seg, "h"), P(seg, "h"), P("h", None))
    out_specs = (P(seg, "h"), P((*seg, "h"), None))
    return jax.shard_map(local, mesh=fine, in_specs=in_specs, out_specs=out_specs, check_vma=False)
```

time: 1610 us -> 101 us (0.06)
  waiting for transfers between devices: 1570 us -> 23.3 us
  starting transfers between devices: 0.16 us -> 45.5 us
  Pallas kernels: 0 us -> 18.7 us
    unnamed x5 -> x0, waiting for transfers between devices: 1290 us -> none
    all_gather x1 -> x0, waiting for transfers between devices: 199 us -> none  [local(): lax.all_gather(proj_test, 'seg', axis=0, tiled=True)]
    psum x1 -> x0, waiting for transfers between devices: 49.7 us -> none  [spread(): return lax.psum(kept, axis)]
    reduce_scatter x1 -> x0, waiting for transfers between devices: 30.9 us -> none  [local(): lax.psum_scatter(train_part, 'feat', scatter_dimension=0, tiled=True)]
    all_to_all x0 -> x3, starting transfers between devices: none -> 23.7 us  [the longest x1 9.99 us: local(): parts = lax.all_to_all(part, ('h', 'l', 'c'), 0, 0, tiled=True)]
    ppermute x0 -> x7, starting transfers between devices: none -> 21.8 us  [the longest x1 7.2 us: local(): sent = lax.ppermute(first, AXES, TO_SECOND_HALF)]
    ppermute x0 -> x7, waiting for transfers between devices: none -> 21.2 us  [the longest x3 10.3 us: local(): lax.ppermute(rows, AXES, ALONG[d])]
    pallas_call x0 -> x8, Pallas kernels: none -> 18.7 us  [the longest x1 6.43 us: scores_of(): pl.pallas_call(scores_kernel, grid=(8,), in_specs=[pl.BlockSpec(memory_sp...]
  transfers between devices with their start and end apart: 4 -> 10, of which waited for: 4 -> 5; matrix products, arithmetic and copies ran while one was open for 0% -> 0% of each run, Pallas kernels for 0% -> 14%
where the time goes in v2:
time: 101 us; the launch traced here: 99.7 us
  starting transfers between devices  45.5 us (45%)
  waiting for transfers between devices  23.3 us (23%)
  Pallas kernels  18.7 us (19%)
  local copies, waits for them, and re-layouts  11.3 us (11%)
    ppermute x3, waiting for transfers between devices, local(): lax.ppermute(rows, AXES, ALONG[d])  10.3 us
    all_to_all x1, starting transfers between devices, local(): parts = lax.all_to_all(part, ('h', 'l', 'c'), 0, 0, tiled=True)  9.99 us
    unnamed x12, local copies, waits for them, and re-layouts  9.72 us
    ppermute x1, waiting for transfers between devices, local(): got = lax.ppermute(give, AXES, OTHER_HALF)  8.65 us
    ppermute x1, starting transfers between devices, local(): sent = lax.ppermute(first, AXES, TO_SECOND_HALF)  7.2 us
    all_to_all x1, starting transfers between devices, local(): rows = lax.all_to_all(rows, ('y', 'x'), 0, 0, tiled=True)  6.93 us
    all_to_all x1, starting transfers between devices, local(): tests = lax.all_to_all(tests, ('y', 'x'), 0, 0, tiled=True)  6.75 us
    pallas_call x1, Pallas kernels, scores_of(): pl.pallas_call(scores_kernel, grid=(8,), in_specs=[pl.BlockSpec(memory_sp...  6.43 us
  transfers between devices with their start and end apart: 10, of which 5 were waited for; matrix products, arithmetic and copies ran while one was open for 0% of the time, Pallas kernels for 14%

profile of v2, /device:TPU:1, one launch (start us, length us, event | category | flops | bytes accessed | tf_op | source)
XLA Modules:
  0.0 99.7 jit_solution(7843473521592831127)
XLA Ops:
  0.6 1.0 slice.3.after_ref
  1.6 0.0 copy-start.3
  1.6 1.6 %copy-done.3 = bf16[4096,256]{1,0:T(8,128)(2,1)S(1)} copy-done((bf16[4096,256]{1,0:T(8,128)(2,1)S(1)}, bf16[4096,256]{1,0:T(8,128)(2,1)}, u32[]{:S(2)}) %copy-start.3) | copy-done | bytes 2097176
  3.2 1.0 %copy-done.4 = bf16[64,4096]{1,0:T(8,128)(2,1)S(1)} copy-done((bf16[64,4096]{1,0:T(8,128)(2,1)S(1)}, bf16[64,4096]{1,0:T(8,128)(2,1)}, u32[]{:S(2)}) %copy-start.4) | copy-done | bytes 524312
  4.2 1.9 %test_parts.1 = (bf16[16,64,128]{2,1,0:T(8,128)(2,1)}, bf16[4096,256]{1,0:T(8,128)(2,1)S(1)}) custom-call(bf16[64,4096]{1,0:T(8,128)(2,1)S(1)} %copy-done.4, bf16[4096,256]{1,0:T(8,128)(2,1)S(1)} %copy-done.3, bf16[512,256]{1,0:T(8,128)(2,1)S(1)} %slice.3.after_ref), custom_call_target="tpu_custom_call" | custom-call | flops 134217728 | bytes 5242880 | tf_op jit(solution)/shard_map/test_parts/pallas_call | solution.py:76
  6.2 10.0 %all-to-all-start = ((bf16[16,64,128]{2,1,0:T(8,128)(2,1)}), bf16[16,64,128]{2,1,0:T(8,128)(2,1)S(1)}, u32[]{:S(2)}, u32[]{:S(2)}) async-start(bf16[16,64,128]{2,1,0:T(8,128)(2,1)} %get-tuple-element.22), calls=%async_computation | async-start | bytes 524288 | tf_op jit(solution)/shard_map/all_to_all | solution.py:291
  16.2 7.2 %collective-permute-start = (bf16[512,256]{1,0:T(8,128)(2,1)S(1)}, bf16[512,256]{1,0:T(8,128)(2,1)S(1)}, u32[]{:S(2)}, u32[]{:S(2)}) collective-permute-start(bf16[512,256]{1,0:T(8,128)(2,1)S(1)} %slice.3.after_ref), channel_id=1, source_target_pairs={{0,1},{2,3},{4,5},{6,7},{8,9},{10,11},{12,13},{14,15},{16,17},{18,... | collective-permute-start | bytes 786440 | tf_op jit(solution)/shard_map/ppermute | solution.py:289
  23.4 0.1 pad_add_fusion.at_ref
  23.5 2.2 %copy-done = bf16[512,4096]{1,0:T(8,128)(2,1)S(1)} copy-done((bf16[512,4096]{1,0:T(8,128)(2,1)S(1)}, bf16[512,4096]{1,0:T(8,128)(2,1)}, u32[]{:S(2)}) %copy-start) | copy-done | bytes 4194328
  25.6 4.2 %train_parts.1 = (f32[256,256]{1,0:T(8,128)S(1)}, bf16[256,256]{1,0:T(8,128)(2,1)S(1)}, bf16[512,4096]{1,0:T(8,128)(2,1)S(1)}) custom-call(s32[3]{0:T(128)S(1)} %pad_add_fusion.at_ref, bf16[512,4096]{1,0:T(8,128)(2,1)S(1)} %copy-done, bf16[4096,256]{1,0:T(8,128)(2,1)S(1)} %get-tuple-element.23.factor_ref), custom_call_target="tpu_custom_call" | custom-call | flops 1073741824 | bytes 9437184 | tf_op jit(solution)/shard_map/train_parts/pallas_call | solution.py:228
  29.9 2.0 %copy-done.1 = bf16[512,4096]{1,0:T(8,128)(2,1)} copy-done((bf16[512,4096]{1,0:T(8,128)(2,1)}, bf16[512,4096]{1,0:T(8,128)(2,1)S(1)}, u32[]{:S(2)}) %copy-start.1) | copy-done | bytes 4194328
  31.9 0.7 copy-done.5
  32.6 3.0 %spread.1 = bf16[16,512,128]{2,1,0:T(8,128)(2,1)} custom-call(bf16[16,64,128]{2,1,0:T(8,128)(2,1)} %copy-done.5), custom_call_target="tpu_custom_call" | custom-call | flops 1048576 | bytes 2097152 | tf_op jit(solution)/shard_map/spread/pallas_call | solution.py:136
  35.6 6.8 %all-to-all-start.1 = ((bf16[16,512,128]{2,1,0:T(8,128)(2,1)}), bf16[16,512,128]{2,1,0:T(8,128)(2,1)S(1)}, u32[]{:S(2)}, u32[]{:S(2)}) async-start(bf16[16,512,128]{2,1,0:T(8,128)(2,1)} %spread.1), calls=%async_computation.1 | async-start | bytes 4194304 | tf_op jit(solution)/shard_map/all_to_all | solution.py:302
  42.4 2.2 %copy-done.2 = bf16[512,4096]{1,0:T(8,128)(2,1)S(1)} copy-done((bf16[512,4096]{1,0:T(8,128)(2,1)S(1)}, bf16[512,4096]{1,0:T(8,128)(2,1)}, u32[]{:S(2)}) %copy-start.2) | copy-done | bytes 4194328
  44.6 2.0 %gram_terms.1 = (f32[16,256,128]{2,1,0:T(8,128)S(1)}, bf16[16,256,128]{2,1,0:T(8,128)(2,1)S(1)}) custom-call(s32[3]{0:T(128)S(1)} %pad_add_fusion.at_ref, bf16[512,256]{1,0:T(8,128)(2,1)S(1)} %collective-permute-done.got_ref, bf16[512,4096]{1,0:T(8,128)(2,1)S(1)} %copy-done.2), custom_call_target="tpu_custom_call" | custom-call | flops 1073741824 | bytes 7340032 | tf_op jit(solution)/shard_map/gram_terms/pallas_call | solution.py:110
  46.5 1.0 %collective-permute-start.1 = (bf16[16,256,128]{2,1,0:T(8,128)(2,1)S(1)}, bf16[16,256,128]{2,1,0:T(8,128)(2,1)S(1)}, u32[]{:S(2)}, u32[]{:S(2)}) collective-permute-start(bf16[16,256,128]{2,1,0:T(8,128)(2,1)S(1)} %get-tuple-element.30), channel_id=1, source_target_pairs={{0,2},{1,3},{2,0},{3,1},{4,6},{5,7},{6,4},{7,5},{8,10},{9,11},{10,... | collective-permute-start | bytes 3145736 | tf_op jit(solution)/shard_map/ppermute | solution.py:299
  47.5 2.3 %collective-permute-done.1.got_ref = bf16[16,256,128]{2,1,0:T(8,128)(2,1)S(1)} collective-permute-done((bf16[16,256,128]{2,1,0:T(8,128)(2,1)S(1)}, bf16[16,256,128]{2,1,0:T(8,128)(2,1)S(1)}, u32[]{:S(2)}, u32[]{:S(2)}) %collective-permute-start.1) | collective-permute-done | bytes 1048608 | tf_op jit(solution)/shard_map/ppermute | solution.py:299
  49.8 0.2 sum_cores.1
  50.1 3.3 %collective-permute-start.2 = (bf16[4,256,128]{2,1,0:T(8,128)(2,1)S(1)}, bf16[4,256,128]{2,1,0:T(8,128)(2,1)S(1)}, u32[]{:S(2)}, u32[]{:S(2)}) collective-permute-start(bf16[4,256,128]{2,1,0:T(8,128)(2,1)S(1)} %get-tuple-element.32), channel_id=1, source_target_pairs={{0,4},{1,5},{2,6},{3,7},{4,8},{5,9},{6,10},{7,11},{8,12},{9,13},{1... | collective-permute-start | bytes 786440 | tf_op jit(solution)/shard_map/ppermute | solution.py:300
  53.4 0.7 collective-permute-start.3
  54.1 2.3 %collective-permute-start.4 = (bf16[4,256,128]{2,1,0:T(8,128)(2,1)S(1)}, bf16[4,256,128]{2,1,0:T(8,128)(2,1)S(1)}, u32[]{:S(2)}, u32[]{:S(2)}) collective-permute-start(bf16[4,256,128]{2,1,0:T(8,128)(2,1)S(1)} %get-tuple-element.34), channel_id=1, source_target_pairs={{0,12},{1,13},{2,14},{3,15},{4,0},{5,1},{6,2},{7,3},{8,4},{9,5},{1... | collective-permute-start | bytes 786440 | tf_op jit(solution)/shard_map/ppermute | solution.py:300
  56.3 6.1 %collective-permute-start.5 = (bf16[256,256]{1,0:T(8,128)(2,1)S(1)}, bf16[256,256]{1,0:T(8,128)(2,1)S(1)}, u32[]{:S(2)}, u32[]{:S(2)}) collective-permute-start(bf16[256,256]{1,0:T(8,128)(2,1)S(1)} %get-tuple-element.35), channel_id=1, source_target_pairs={{0,1},{1,0},{2,3},{3,2},{4,5},{5,4},{6,7},{7,6},{8,9},{9,8},{10,11... | collective-permute-start | bytes 393224 | tf_op jit(solution)/shard_map/ppermute | solution.py:294
  62.5 9.9 %collective-permute-done.3.b_ref = bf16[4,256,128]{2,1,0:T(8,128)(2,1)S(1)} collective-permute-done((bf16[4,256,128]{2,1,0:T(8,128)(2,1)S(1)}, bf16[4,256,128]{2,1,0:T(8,128)(2,1)S(1)}, u32[]{:S(2)}, u32[]{:S(2)}) %collective-permute-start.3) | collective-permute-done | bytes 262176 | tf_op jit(solution)/shard_map/ppermute | solution.py:300
  72.4 0.4 collective-permute-done.4.d_ref
  72.8 1.0 sum_line.1
  73.7 8.7 %collective-permute-done.5.got_ref = bf16[256,256]{1,0:T(8,128)(2,1)S(1)} collective-permute-done((bf16[256,256]{1,0:T(8,128)(2,1)S(1)}, bf16[256,256]{1,0:T(8,128)(2,1)S(1)}, u32[]{:S(2)}, u32[]{:S(2)}) %collective-permute-start.5) | collective-permute-done | bytes 131104 | tf_op jit(solution)/shard_map/ppermute | solution.py:294
  82.4 1.2 %collective-permute-start.6 = (bf16[16,512,128]{2,1,0:T(8,128)(2,1)S(1)}, bf16[16,512,128]{2,1,0:T(8,128)(2,1)}, u32[]{:S(2)}, u32[]{:S(2)}) collective-permute-start(bf16[16,512,128]{2,1,0:T(8,128)(2,1)S(1)} %all-to-all-done.1.own_ref), channel_id=1, source_target_pairs={{0,2},{1,3},{2,0},{3,1},{4,6},{5,7},{6,4},{7,5},{8,10},{9,11},{10,... | collective-permute-start | bytes 6291464 | tf_op jit(solution)/shard_map/ppermute | solution.py:305
  83.6 6.9 %all-to-all-start.2 = ((bf16[16,64,128]{2,1,0:T(8,128)(2,1)}), bf16[16,64,128]{2,1,0:T(8,128)(2,1)S(1)}, u32[]{:S(2)}, u32[]{:S(2)}) async-start(bf16[16,64,128]{2,1,0:T(8,128)(2,1)} %sum_line.1), calls=%async_computation.2 | async-start | bytes 524288 | tf_op jit(solution)/shard_map/all_to_all | solution.py:306
  90.5 6.4 %scores.1 = bf16[256,8192]{1,0:T(8,128)(2,1)} custom-call(s32[3]{0:T(128)S(1)} %pad_add_fusion.at_ref, f32[256,256]{1,0:T(8,128)S(1)} %get-tuple-element.37.keep_ref, bf16[256,256]{1,0:T(8,128)(2,1)S(1)} %collective-permute-done.5.got_ref, bf16[16,512,128]{2,1,0:T(8,128)(2,1)S(1)} %all-to-all-done.1.own_ref, ...), custom_call_target="tpu_custom_call" | custom-call | flops 1073741824 | bytes 8388608 | tf_op jit(solution)/shard_map/scores/pallas_call | solution.py:272
  97.0 2.1 %all-to-all-done.2.in_ref = bf16[16,64,128]{2,1,0:T(8,128)(2,1)S(1)} async-done(((bf16[16,64,128]{2,1,0:T(8,128)(2,1)}), bf16[16,64,128]{2,1,0:T(8,128)(2,1)S(1)}, u32[]{:S(2)}, u32[]{:S(2)}) %all-to-all-start.2) | async-done | bytes 262176 | tf_op jit(solution)/shard_map/all_to_all | solution.py:306
  99.1 0.6 reshape.7
  (11 shorter events, 0.1 us)
Async XLA Ops:
  1.6 1.6 %copy-start.3 = (bf16[4096,256]{1,0:T(8,128)(2,1)S(1)}, bf16[4096,256]{1,0:T(8,128)(2,1)}, u32[]{:S(2)}) copy-start(bf16[4096,256]{1,0:T(8,128)(2,1)} %factor_ref.1) | copy-start | bytes 6291460
  3.2 1.0 %copy-start.4 = (bf16[64,4096]{1,0:T(8,128)(2,1)S(1)}, bf16[64,4096]{1,0:T(8,128)(2,1)}, u32[]{:S(2)}) copy-start(bf16[64,4096]{1,0:T(8,128)(2,1)} %test_ref.1) | copy-start | bytes 1572868
  6.2 25.7 %all-to-all-start = ((bf16[16,64,128]{2,1,0:T(8,128)(2,1)}), bf16[16,64,128]{2,1,0:T(8,128)(2,1)S(1)}, u32[]{:S(2)}, u32[]{:S(2)}) async-start(bf16[16,64,128]{2,1,0:T(8,128)(2,1)} %get-tuple-element.22), calls=%async_computation | async-start | bytes 524288 | tf_op jit(solution)/shard_map/all_to_all | solution.py:291
  16.2 15.7 %collective-permute-start = (bf16[512,256]{1,0:T(8,128)(2,1)S(1)}, bf16[512,256]{1,0:T(8,128)(2,1)S(1)}, u32[]{:S(2)}, u32[]{:S(2)}) collective-permute-start(bf16[512,256]{1,0:T(8,128)(2,1)S(1)} %slice.3.after_ref), channel_id=1, source_target_pairs={{0,1},{2,3},{4,5},{6,7},{8,9},{10,11},{12,13},{14,15},{16,17},{18,... | collective-permute-start | bytes 786440 | tf_op jit(solution)/shard_map/ppermute | solution.py:289
  23.4 2.2 %copy-start = (bf16[512,4096]{1,0:T(8,128)(2,1)S(1)}, bf16[512,4096]{1,0:T(8,128)(2,1)}, u32[]{:S(2)}) copy-start(bf16[512,4096]{1,0:T(8,128)(2,1)} %train_ref.1) | copy-start | bytes 12582916
  29.9 2.0 %copy-start.1 = (bf16[512,4096]{1,0:T(8,128)(2,1)}, bf16[512,4096]{1,0:T(8,128)(2,1)S(1)}, u32[]{:S(2)}) copy-start(bf16[512,4096]{1,0:T(8,128)(2,1)S(1)} %get-tuple-element.28.train_ref) | copy-start | bytes 12582916
  31.9 0.7 copy-start.5
  35.6 46.8 %all-to-all-start.1 = ((bf16[16,512,128]{2,1,0:T(8,128)(2,1)}), bf16[16,512,128]{2,1,0:T(8,128)(2,1)S(1)}, u32[]{:S(2)}, u32[]{:S(2)}) async-start(bf16[16,512,128]{2,1,0:T(8,128)(2,1)} %spread.1), calls=%async_computation.1 | async-start | bytes 4194304 | tf_op jit(solution)/shard_map/all_to_all | solution.py:302
  42.4 2.2 %copy-start.2 = (bf16[512,4096]{1,0:T(8,128)(2,1)S(1)}, bf16[512,4096]{1,0:T(8,128)(2,1)}, u32[]{:S(2)}) copy-start(bf16[512,4096]{1,0:T(8,128)(2,1)} %copy-done.1) | copy-start | bytes 12582916
  46.5 3.3 %collective-permute-start.1 = (bf16[16,256,128]{2,1,0:T(8,128)(2,1)S(1)}, bf16[16,256,128]{2,1,0:T(8,128)(2,1)S(1)}, u32[]{:S(2)}, u32[]{:S(2)}) collective-permute-start(bf16[16,256,128]{2,1,0:T(8,128)(2,1)S(1)} %get-tuple-element.30), channel_id=1, source_target_pairs={{0,2},{1,3},{2,0},{3,1},{4,6},{5,7},{6,4},{7,5},{8,10},{9,11},{10,... | collective-permute-start | bytes 3145736 | tf_op jit(solution)/shard_map/ppermute | solution.py:299
  50.1 12.4 %collective-permute-start.2 = (bf16[4,256,128]{2,1,0:T(8,128)(2,1)S(1)}, bf16[4,256,128]{2,1,0:T(8,128)(2,1)S(1)}, u32[]{:S(2)}, u32[]{:S(2)}) collective-permute-start(bf16[4,256,128]{2,1,0:T(8,128)(2,1)S(1)} %get-tuple-element.32), channel_id=1, source_target_pairs={{0,4},{1,5},{2,6},{3,7},{4,8},{5,9},{6,10},{7,11},{8,12},{9,13},{1... | collective-permute-start | bytes 786440 | tf_op jit(solution)/shard_map/ppermute | solution.py:300
  53.4 19.0 %collective-permute-start.3 = (bf16[4,256,128]{2,1,0:T(8,128)(2,1)S(1)}, bf16[4,256,128]{2,1,0:T(8,128)(2,1)S(1)}, u32[]{:S(2)}, u32[]{:S(2)}) collective-permute-start(bf16[4,256,128]{2,1,0:T(8,128)(2,1)S(1)} %get-tuple-element.33), channel_id=1, source_target_pairs={{0,8},{1,9},{2,10},{3,11},{4,12},{5,13},{6,14},{7,15},{8,0},{9,1},... | collective-permute-start | bytes 786440 | tf_op jit(solution)/shard_map/ppermute | solution.py:300
  54.1 18.7 %collective-permute-start.4 = (bf16[4,256,128]{2,1,0:T(8,128)(2,1)S(1)}, bf16[4,256,128]{2,1,0:T(8,128)(2,1)S(1)}, u32[]{:S(2)}, u32[]{:S(2)}) collective-permute-start(bf16[4,256,128]{2,1,0:T(8,128)(2,1)S(1)} %get-tuple-element.34), channel_id=1, source_target_pairs={{0,12},{1,13},{2,14},{3,15},{4,0},{5,1},{6,2},{7,3},{8,4},{9,5},{1... | collective-permute-start | bytes 786440 | tf_op jit(solution)/shard_map/ppermute | solution.py:300
  56.3 26.0 %collective-permute-start.5 = (bf16[256,256]{1,0:T(8,128)(2,1)S(1)}, bf16[256,256]{1,0:T(8,128)(2,1)S(1)}, u32[]{:S(2)}, u32[]{:S(2)}) collective-permute-start(bf16[256,256]{1,0:T(8,128)(2,1)S(1)} %get-tuple-element.35), channel_id=1, source_target_pairs={{0,1},{1,0},{2,3},{3,2},{4,5},{5,4},{6,7},{7,6},{8,9},{9,8},{10,11... | collective-permute-start | bytes 393224 | tf_op jit(solution)/shard_map/ppermute | solution.py:294
  82.4 8.1 %collective-permute-start.6 = (bf16[16,512,128]{2,1,0:T(8,128)(2,1)S(1)}, bf16[16,512,128]{2,1,0:T(8,128)(2,1)}, u32[]{:S(2)}, u32[]{:S(2)}) collective-permute-start(bf16[16,512,128]{2,1,0:T(8,128)(2,1)S(1)} %all-to-all-done.1.own_ref), channel_id=1, source_target_pairs={{0,2},{1,3},{2,0},{3,1},{4,6},{5,7},{6,4},{7,5},{8,10},{9,11},{10,... | collective-permute-start | bytes 6291464 | tf_op jit(solution)/shard_map/ppermute | solution.py:305
  83.6 15.5 %all-to-all-start.2 = ((bf16[16,64,128]{2,1,0:T(8,128)(2,1)}), bf16[16,64,128]{2,1,0:T(8,128)(2,1)S(1)}, u32[]{:S(2)}, u32[]{:S(2)}) async-start(bf16[16,64,128]{2,1,0:T(8,128)(2,1)} %sum_line.1), calls=%async_computation.2 | async-start | bytes 524288 | tf_op jit(solution)/shard_map/all_to_all | solution.py:306

commit v3 on v2

v3 whole, which is shorter than its diff:
```python
import math

import jax
import jax.numpy as jnp
from jax import lax
from jax.experimental import pallas as pl
from jax.experimental.pallas import tpu as pltpu
from jax.sharding import Mesh, PartitionSpec as P

W = 256
AXES = ("y", "x", "l", "c", "h")
SIZES = (4, 4, 4, 2, 2)
MIB = 1 << 20
BIG = 56
BF16, F32 = jnp.bfloat16, jnp.float32


def pairs(move, keep=None):
    out = []
    for i in range(math.prod(SIZES)):
        h, c, l, yx = i % 2, i // 2 % 2, i // 4 % 4, i // 16
        if keep is None or keep(l, c, h):
            l2, c2, h2 = move(l, c, h)
            out.append((i, ((yx * 4 + l2) * 2 + c2) * 2 + h2))
    return out


OTHER_HALF = pairs(lambda l, c, h: (l, c, 1 - h))
TO_SECOND_HALF = pairs(lambda l, c, h: (l, c, 1), lambda l, c, h: h == 0)
OTHER_CORE = pairs(lambda l, c, h: (l, 1 - c, h))
ALONG = [pairs(lambda l, c, h, d=d: ((l + d) % 4, c, h)) for d in range(4)]


def params(mib):
    return pltpu.CompilerParams(vmem_limit_bytes=mib * MIB)


def cost(flops, nbytes):
    return pl.CostEstimate(flops=flops, bytes_accessed=nbytes, transcendentals=0)


def anywhere():
    return pl.BlockSpec(memory_space=pltpu.HBM)


def whole():
    return pl.BlockSpec(memory_space=pltpu.VMEM)


def test_kernel(test_ref, factor_ref, keep_ref, give_ref):
    total = jnp.dot(test_ref[...], factor_ref[...], preferred_element_type=F32)
    keep_ref[...] = total
    give_ref[...] = total.astype(BF16)


def test_parts(test_feats, factor_panel):
    return pl.pallas_call(
        test_kernel,
        in_specs=[whole()] * 2,
        out_specs=[whole()] * 2,
        out_shape=[jax.ShapeDtypeStruct((64, 256), F32), jax.ShapeDtypeStruct((64, 256), BF16)],
        compiler_params=params(8),
        cost_estimate=cost(2 * 64 * 4096 * 256, 3 * MIB),
        name="test_parts",
    )(test_feats, factor_panel)


def gram_kernel(at_ref, got_ref, train_ref, mine_ref, theirs_ref):
    l, c, h = at_ref[0], at_ref[1], at_ref[2]
    place = lax.broadcasted_iota(jnp.int32, (256, 256), 0)
    column = lax.broadcasted_iota(jnp.int32, (256, 256), 1)
    yx, l_of, c_of = (place >> 3) & 15, (l + (place >> 1)) & 3, (c + (place >> 7)) & 1
    wanted = (yx << 4) + (l_of << 2) + (c_of << 1) + (place & 1)
    choose = jnp.where(wanted == column, 1.0, 0.0).astype(BF16)
    panel = jnp.where(h == 0, train_ref[:, :W].astype(F32), got_ref[...].astype(F32)).astype(BF16)
    panel = lax.dot_general(choose, panel, (((1,), (1,)), ((), ())), preferred_element_type=F32)
    panel = panel.astype(BF16)
    for i in range(8):
        term = jnp.dot(panel, train_ref[:, 512 * i : 512 * i + 512], preferred_element_type=F32)
        blocks = [term[:, 128 * t : 128 * t + 128].reshape(32, 8, 128) for t in range(4)]
        term = jnp.concatenate(blocks, axis=1)
        mine_ref[:, 32 * i : 32 * i + 32, :] = term[:16]
        theirs_ref[:, 32 * i : 32 * i + 32, :] = term[16:].astype(BF16)


def gram_terms(at, got, train_feats):
    return pl.pallas_call(
        gram_kernel,
        in_specs=[pl.BlockSpec(memory_space=pltpu.SMEM), whole(), whole()],
        out_specs=[whole()] * 2,
        out_shape=[
            jax.ShapeDtypeStruct((16, 256, 128), F32),
            jax.ShapeDtypeStruct((16, 256, 128), BF16),
        ],
        compiler_params=params(16),
        cost_estimate=cost(2 * 256 * 512 * 4096, 7 * MIB),
        name="gram_terms",
    )(at, got, train_feats)


def halves_kernel(keep_ref, got_ref, out_ref):
    proj = (keep_ref[...] + got_ref[...].astype(F32)).astype(BF16)
    for dest in range(8):
        out_ref[dest] = proj[:, 128 * (dest % 2) : 128 * (dest % 2) + 128]


def sum_halves(keep, got):
    return pl.pallas_call(
        halves_kernel,
        in_specs=[whole()] * 2,
        out_specs=whole(),
        out_shape=jax.ShapeDtypeStruct((8, 64, 128), BF16),
        compiler_params=params(8),
        cost_estimate=cost(1 << 16, MIB // 4),
        name="sum_halves",
    )(keep, got)


def spread_kernel(parts_ref, out_ref):
    proj = parts_ref[...].astype(F32).reshape(4, 128, 128)
    proj = jnp.concatenate([proj[l].T for l in range(4)], axis=0).astype(BF16)
    for dest in range(16):
        out_ref[dest] = proj


def spread(parts):
    return pl.pallas_call(
        spread_kernel,
        in_specs=[whole()],
        out_specs=whole(),
        out_shape=jax.ShapeDtypeStruct((16, 512, 128), BF16),
        compiler_params=params(8),
        cost_estimate=cost(MIB, 2 * MIB),
        name="spread",
    )(parts)


def cores_kernel(mine_ref, got_ref, out_ref):
    out_ref[...] = (mine_ref[...] + got_ref[...].astype(F32)).astype(BF16)


def sum_cores(mine, got):
    return pl.pallas_call(
        cores_kernel,
        in_specs=[whole()] * 2,
        out_specs=whole(),
        out_shape=jax.ShapeDtypeStruct((16, 256, 128), BF16),
        compiler_params=params(8),
        cost_estimate=cost(MIB // 2, 4 * MIB),
        name="sum_cores",
    )(mine, got)


def fold_kernel(in_ref, own_ref, a_ref, b_ref, d_ref, sum_ref):
    total = in_ref[0].astype(F32)
    for s in range(1, 16):
        total = total + in_ref[s].astype(F32)
    sum_ref[...] = total
    for step, ref in enumerate((own_ref, a_ref, b_ref, d_ref)):
        for j in range(2):
            rows = sum_ref[pl.ds(2 * step + j, 32, stride=8), :]
            ref[32 * j : 32 * j + 32, :] = rows.astype(ref.dtype)


def fold(rows):
    return pl.pallas_call(
        fold_kernel,
        in_specs=[whole()],
        out_specs=[whole()] * 4,
        out_shape=[jax.ShapeDtypeStruct((64, 128), F32)] + [jax.ShapeDtypeStruct((64, 128), BF16)] * 3,
        scratch_shapes=[pltpu.VMEM((256, 128), F32)],
        compiler_params=params(8),
        cost_estimate=cost(MIB // 2, MIB),
        name="fold",
    )(rows)


def train_kernel(at_ref, train_ref, factor_ref, keep_ref, give_ref, sum_ref):
    for n in range(4):
        rows = slice(128 * n, 128 * n + 128)
        sum_ref[rows, :] = jnp.dot(train_ref[rows, :], factor_ref[...], preferred_element_type=F32)
    h = at_ref[2]
    keep_ref[...] = sum_ref[pl.ds(pl.multiple_of(256 * h, 256), 256), :]
    give_ref[...] = sum_ref[pl.ds(pl.multiple_of(256 - 256 * h, 256), 256), :].astype(BF16)


def train_parts(at, train_feats, factor_panel):
    return pl.pallas_call(
        train_kernel,
        in_specs=[pl.BlockSpec(memory_space=pltpu.SMEM), whole(), whole()],
        out_specs=[whole()] * 2,
        out_shape=[jax.ShapeDtypeStruct((256, 256), F32), jax.ShapeDtypeStruct((256, 256), BF16)],
        scratch_shapes=[pltpu.VMEM((512, 256), F32)],
        compiler_params=params(8),
        cost_estimate=cost(2 * 512 * 4096 * 256, 7 * MIB),
        name="train_parts",
    )(at, train_feats, factor_panel)


def scores_kernel(at_ref, keep_ref, got_ref, own_ref, other_ref, out_ref, made_ref, sem):
    c = at_ref[1]
    proj = keep_ref[...] + got_ref[...].astype(F32)
    low, high = proj[:, :128], proj[:, 128:]
    proj = jnp.concatenate([jnp.where(c == 0, low, high), jnp.where(c == 0, high, low)], axis=1)
    proj = proj.astype(BF16)
    copies = []
    for n in range(32):
        tests = jnp.concatenate(
            [
                jnp.concatenate(
                    [
                        ref[n // 2, 256 * (n % 2) + 128 * t : 256 * (n % 2) + 128 * t + 128, :]
                        for t in range(2)
                    ],
                    axis=1,
                )
                for ref in (own_ref, other_ref)
            ],
            axis=0,
        )
        product = jnp.dot(proj, tests, preferred_element_type=F32)
        made_ref[:, 256 * n : 256 * n + 256] = (product * (1.0 / math.sqrt(256))).astype(BF16)
        if n % 4 == 3:
            done = pl.ds(256 * (n - 3), 1024)
            copies.append(
                pltpu.make_async_copy(made_ref.at[:, done], out_ref.at[:, done], sem.at[n // 4])
            )
            copies[-1].start()
    for copy in copies:
        copy.wait()


def scores_of(at, keep, got, own, other):
    return pl.pallas_call(
        scores_kernel,
        in_specs=[pl.BlockSpec(memory_space=pltpu.SMEM)] + [whole()] * 4,
        out_specs=anywhere(),
        out_shape=jax.ShapeDtypeStruct((256, 8192), BF16),
        scratch_shapes=[pltpu.VMEM((256, 8192), BF16), pltpu.SemaphoreType.DMA((8,))],
        compiler_params=params(16),
        cost_estimate=cost(1 << 30, 8 * MIB),
        name="scores",
    )(at, keep, got, own, other)


def local(train_feats, test_feats, factor_panel):
    at = jnp.stack([lax.axis_index(a) for a in ("l", "c", "h")]).astype(jnp.int32)

    test_keep, test_give = test_parts(test_feats, factor_panel)
    parts = sum_halves(test_keep, lax.ppermute(test_give, AXES, OTHER_HALF))
    keep, give = train_parts(at, train_feats, factor_panel)
    parts, give = lax.optimization_barrier((parts, give))
    parts = lax.all_to_all(parts, ("l", "c"), 0, 0, tiled=True)
    parts, first = lax.optimization_barrier((parts, train_feats[:, :W]))
    tests = spread(parts)

    sent = lax.ppermute(first, AXES, TO_SECOND_HALF)
    sent, give, _ = lax.optimization_barrier((sent, give, tests))
    got = lax.ppermute(give, AXES, OTHER_HALF)
    mine, theirs = gram_terms(at, sent, train_feats)
    rows = sum_cores(mine, lax.ppermute(theirs, AXES, OTHER_CORE))
    tests = lax.all_to_all(tests, ("y", "x"), 0, 0, tiled=True)
    tests, rows, got = lax.optimization_barrier((tests, rows, got))

    other = lax.ppermute(tests, AXES, OTHER_CORE)
    rows = lax.all_to_all(rows, ("y", "x"), 0, 0, tiled=True)
    scores = scores_of(at, keep, got, tests, other)
    rows, scores = lax.optimization_barrier((rows, scores))
    total, *sums = fold(rows)
    for d, block in enumerate(sums, 1):
        total = total + lax.ppermute(block, AXES, ALONG[d]).astype(F32)
    gram_panel = total.reshape(2, 4096) / 65536
    return (gram_panel, scores)


def solution(mesh):
    fine = Mesh(mesh.devices.reshape(SIZES), AXES)
    seg = ("y", "x", "l", "c")
    in_specs = (P(seg, "h"), P(seg, "h"), P("h", None))
    out_specs = (P(seg, "h"), P((*seg, "h"), None))
    return jax.shard_map(local, mesh=fine, in_specs=in_specs, out_specs=out_specs, check_vma=False)
```

time: 101 us -> 98.3 us (0.973)
  Pallas kernels: 18.7 us -> 9.56 us
  waiting for transfers between devices: 23.3 us -> 32.2 us
  starting transfers between devices: 45.5 us -> 43.2 us
    all_to_all x1, waiting for transfers between devices: 2.1 us -> 15 us  [local(): rows = lax.all_to_all(rows, ('y', 'x'), 0, 0, tiled=True)]
    ppermute x4 -> x5, waiting for transfers between devices: 12.6 us -> 1.6 us  [the longest x3 1.6 us: local(): total = total + lax.ppermute(block, AXES, ALONG[d]).astype(F32)]
    ppermute x4 -> x5, starting transfers between devices: 7.3 us -> 14.6 us  [the longest x1 7.83 us: local(): parts = sum_halves(test_keep, lax.ppermute(test_give, AXES, OTHER_HALF))]
    pallas_call x6, Pallas kernels: 12.6 us -> 5.79 us  [the longest x1 3.97 us: scores_of(): pl.pallas_call(scores_kernel, in_specs=[pl.BlockSpec(memory_space=pltpu.S...]
    ppermute x1, waiting for transfers between devices: 8.65 us -> 2.58 us  [local(): got = lax.ppermute(give, AXES, OTHER_HALF)]
    all_to_all x1, starting transfers between devices: 9.99 us -> 4.24 us  [local(): parts = lax.all_to_all(parts, ('l', 'c'), 0, 0, tiled=True)]
    all_to_all x1, waiting for transfers between devices: 0.01 us -> 4.87 us  [local(): parts = lax.all_to_all(parts, ('l', 'c'), 0, 0, tiled=True)]
    ppermute x1, waiting for transfers between devices: 0.01 us -> 4.31 us  [local(): sent = lax.ppermute(first, AXES, TO_SECOND_HALF)]
  transfers between devices with their start and end apart: 10 -> 11, of which waited for: 5 -> 7; matrix products, arithmetic and copies ran while one was open for 0% -> 1% of each run, Pallas kernels for 14% -> 8%
where the time goes in v3:
time: 98.3 us; the launch traced here: 96.8 us
  starting transfers between devices  43.2 us (44%)
  waiting for transfers between devices  32.2 us (33%)
  local copies, waits for them, and re-layouts  10.9 us (11%)
  Pallas kernels  9.56 us (10%)
    all_to_all x1, waiting for transfers between devices, local(): rows = lax.all_to_all(rows, ('y', 'x'), 0, 0, tiled=True)  15 us
    unnamed x14, local copies, waits for them, and re-layouts  9.31 us
    ppermute x1, starting transfers between devices, local(): parts = sum_halves(test_keep, lax.ppermute(test_give, AXES, OTHER_HALF))  7.83 us
    all_to_all x1, starting transfers between devices, local(): tests = lax.all_to_all(tests, ('y', 'x'), 0, 0, tiled=True)  6.75 us
    ppermute x1, starting transfers between devices, local(): got = lax.ppermute(give, AXES, OTHER_HALF)  6.23 us
    ppermute x1, starting transfers between devices, local(): sent = lax.ppermute(first, AXES, TO_SECOND_HALF)  5.34 us
    all_to_all x1, waiting for transfers between devices, local(): parts = lax.all_to_all(parts, ('l', 'c'), 0, 0, tiled=True)  4.87 us
    ppermute x3, starting transfers between devices, local(): total = total + lax.ppermute(block, AXES, ALONG[d]).astype(F32)  4.51 us
  transfers between devices with their start and end apart: 11, of which 7 were waited for; matrix products, arithmetic and copies ran while one was open for 1% of the time, Pallas kernels for 8%

profile of v3, /device:TPU:1, one launch (start us, length us, event | category | flops | bytes accessed | tf_op | source)
XLA Modules:
  0.0 96.8 jit_solution(17550773231168934461)
XLA Ops:
  0.6 1.6 %copy-done.2 = bf16[4096,256]{1,0:T(8,128)(2,1)S(1)} copy-done((bf16[4096,256]{1,0:T(8,128)(2,1)S(1)}, bf16[4096,256]{1,0:T(8,128)(2,1)}, u32[]{:S(2)}) %copy-start.2) | copy-done | bytes 2097176
  2.2 1.0 %copy-done.6 = bf16[64,4096]{1,0:T(8,128)(2,1)S(1)} copy-done((bf16[64,4096]{1,0:T(8,128)(2,1)S(1)}, bf16[64,4096]{1,0:T(8,128)(2,1)}, u32[]{:S(2)}) %copy-start.6) | copy-done | bytes 524312
  3.3 0.5 test_parts.1
  3.8 7.8 %collective-permute-start = (bf16[64,256]{1,0:T(8,128)(2,1)S(1)}, bf16[64,256]{1,0:T(8,128)(2,1)S(1)}, u32[]{:S(2)}, u32[]{:S(2)}) collective-permute-start(bf16[64,256]{1,0:T(8,128)(2,1)S(1)} %get-tuple-element.24), channel_id=1, source_target_pairs={{0,1},{1,0},{2,3},{3,2},{4,5},{5,4},{6,7},{7,6},{8,9},{9,8},{10,11... | collective-permute-start | bytes 98312 | tf_op jit(solution)/shard_map/ppermute | solution.py:250
  11.7 2.2 %copy-done = bf16[512,4096]{1,0:T(8,128)(2,1)S(1)} copy-done((bf16[512,4096]{1,0:T(8,128)(2,1)S(1)}, bf16[512,4096]{1,0:T(8,128)(2,1)}, u32[]{:S(2)}) %copy-start) | copy-done | bytes 4194328
  13.8 1.8 %train_parts.1 = (f32[256,256]{1,0:T(8,128)S(1)}, bf16[256,256]{1,0:T(8,128)(2,1)S(1)}) custom-call(s32[3]{0:T(128)S(1)} %pad_add_fusion.at_ref, bf16[512,4096]{1,0:T(8,128)(2,1)S(1)} %copy-done, bf16[4096,256]{1,0:T(8,128)(2,1)S(1)} %copy-done.3), custom_call_target="tpu_custom_call" | custom-call | flops 1073741824 | bytes 7340032 | tf_op jit(solution)/shard_map/train_parts/pallas_call | solution.py:188
  15.7 0.7 sum_halves.1
  16.4 4.2 %all-to-all-start = ((bf16[8,64,128]{2,1,0:T(8,128)(2,1)}), bf16[8,64,128]{2,1,0:T(8,128)(2,1)S(1)}, u32[]{:S(2)}, u32[]{:S(2)}) async-start(bf16[8,64,128]{2,1,0:T(8,128)(2,1)} %sum_halves.1), calls=%async_computation | async-start | bytes 262144 | tf_op jit(solution)/shard_map/all_to_all | solution.py:253
  20.6 1.0 slice.3
  21.6 4.9 %all-to-all-done.parts_ref = bf16[8,64,128]{2,1,0:T(8,128)(2,1)S(1)} async-done(((bf16[8,64,128]{2,1,0:T(8,128)(2,1)}), bf16[8,64,128]{2,1,0:T(8,128)(2,1)S(1)}, u32[]{:S(2)}, u32[]{:S(2)}) %all-to-all-start) | async-done | bytes 131104 | tf_op jit(solution)/shard_map/all_to_all | solution.py:253
  26.4 0.3 spread.1
  26.8 1.3 %copy-done.4 = bf16[16,512,128]{2,1,0:T(8,128)(2,1)} copy-done((bf16[16,512,128]{2,1,0:T(8,128)(2,1)}, bf16[16,512,128]{2,1,0:T(8,128)(2,1)S(1)}, u32[]{:S(2)}) %copy-start.4) | copy-done | bytes 2097176
  28.1 6.8 %all-to-all-start.1 = ((bf16[16,512,128]{2,1,0:T(8,128)(2,1)}), bf16[16,512,128]{2,1,0:T(8,128)(2,1)S(1)}, u32[]{:S(2)}, u32[]{:S(2)}) async-start(bf16[16,512,128]{2,1,0:T(8,128)(2,1)} %copy-done.4), calls=%async_computation.1 | async-start | bytes 4194304 | tf_op jit(solution)/shard_map/all_to_all | solution.py:262
  34.8 5.3 %collective-permute-start.1 = (bf16[512,256]{1,0:T(8,128)(2,1)S(1)}, bf16[512,256]{1,0:T(8,128)(2,1)S(1)}, u32[]{:S(2)}, u32[]{:S(2)}) collective-permute-start(bf16[512,256]{1,0:T(8,128)(2,1)S(1)} %slice.3), channel_id=1, source_target_pairs={{0,1},{2,3},{4,5},{6,7},{8,9},{10,11},{12,13},{14,15},{16,17},{18,... | collective-permute-start | bytes 786440 | tf_op jit(solution)/shard_map/ppermute | solution.py:257
  40.2 4.3 %collective-permute-done.1.got_ref = bf16[512,256]{1,0:T(8,128)(2,1)S(1)} collective-permute-done((bf16[512,256]{1,0:T(8,128)(2,1)S(1)}, bf16[512,256]{1,0:T(8,128)(2,1)S(1)}, u32[]{:S(2)}, u32[]{:S(2)}) %collective-permute-start.1) | collective-permute-done | bytes 262176 | tf_op jit(solution)/shard_map/ppermute | solution.py:257
  44.5 2.2 %copy-done.1 = bf16[512,4096]{1,0:T(8,128)(2,1)S(1)} copy-done((bf16[512,4096]{1,0:T(8,128)(2,1)S(1)}, bf16[512,4096]{1,0:T(8,128)(2,1)}, u32[]{:S(2)}) %copy-start.1) | copy-done | bytes 4194328
  46.7 1.9 %gram_terms.1 = (f32[16,256,128]{2,1,0:T(8,128)S(1)}, bf16[16,256,128]{2,1,0:T(8,128)(2,1)S(1)}) custom-call(s32[3]{0:T(128)S(1)} %pad_add_fusion.at_ref, bf16[512,256]{1,0:T(8,128)(2,1)S(1)} %collective-permute-done.1.got_ref, bf16[512,4096]{1,0:T(8,128)(2,1)S(1)} %copy-done.1), custom_call_target="tpu_custom_call" | custom-call | flops 1073741824 | bytes 7340032 | tf_op jit(solution)/shard_map/gram_terms/pallas_call | solution.py:87
  48.6 2.3 %collective-permute-start.2 = (bf16[16,256,128]{2,1,0:T(8,128)(2,1)S(1)}, bf16[16,256,128]{2,1,0:T(8,128)(2,1)S(1)}, u32[]{:S(2)}, u32[]{:S(2)}) collective-permute-start(bf16[16,256,128]{2,1,0:T(8,128)(2,1)S(1)} %get-tuple-element.32), channel_id=1, source_target_pairs={{0,2},{1,3},{2,0},{3,1},{4,6},{5,7},{6,4},{7,5},{8,10},{9,11},{10,... | collective-permute-start | bytes 3145736 | tf_op jit(solution)/shard_map/ppermute | solution.py:261
  50.9 6.2 %collective-permute-start.3 = (bf16[256,256]{1,0:T(8,128)(2,1)S(1)}, bf16[256,256]{1,0:T(8,128)(2,1)S(1)}, u32[]{:S(2)}, u32[]{:S(2)}) collective-permute-start(bf16[256,256]{1,0:T(8,128)(2,1)S(1)} %get-tuple-element.33), channel_id=1, source_target_pairs={{0,1},{1,0},{2,3},{3,2},{4,5},{5,4},{6,7},{7,6},{8,9},{9,8},{10,11... | collective-permute-start | bytes 393224 | tf_op jit(solution)/shard_map/ppermute | solution.py:259
  57.3 1.0 %copy-done.5 = bf16[16,256,128]{2,1,0:T(8,128)(2,1)} copy-done((bf16[16,256,128]{2,1,0:T(8,128)(2,1)}, bf16[16,256,128]{2,1,0:T(8,128)(2,1)S(1)}, u32[]{:S(2)}) %copy-start.5) | copy-done | bytes 1048600
  58.3 2.6 %collective-permute-done.3.got_ref = bf16[256,256]{1,0:T(8,128)(2,1)S(1)} collective-permute-done((bf16[256,256]{1,0:T(8,128)(2,1)S(1)}, bf16[256,256]{1,0:T(8,128)(2,1)S(1)}, u32[]{:S(2)}, u32[]{:S(2)}) %collective-permute-start.3) | collective-permute-done | bytes 131104 | tf_op jit(solution)/shard_map/ppermute | solution.py:259
  60.9 3.6 %all-to-all-done.1.own_ref = bf16[16,512,128]{2,1,0:T(8,128)(2,1)S(1)} async-done(((bf16[16,512,128]{2,1,0:T(8,128)(2,1)}), bf16[16,512,128]{2,1,0:T(8,128)(2,1)S(1)}, u32[]{:S(2)}, u32[]{:S(2)}) %all-to-all-start.1) | async-done | bytes 2097184 | tf_op jit(solution)/shard_map/all_to_all | solution.py:262
  64.5 2.4 %collective-permute-start.4 = (bf16[16,512,128]{2,1,0:T(8,128)(2,1)S(1)}, bf16[16,512,128]{2,1,0:T(8,128)(2,1)}, u32[]{:S(2)}, u32[]{:S(2)}) collective-permute-start(bf16[16,512,128]{2,1,0:T(8,128)(2,1)S(1)} %all-to-all-done.1.own_ref), channel_id=1, source_target_pairs={{0,2},{1,3},{2,0},{3,1},{4,6},{5,7},{6,4},{7,5},{8,10},{9,11},{10,... | collective-permute-start | bytes 6291464 | tf_op jit(solution)/shard_map/ppermute | solution.py:265
  66.9 3.7 %all-to-all-start.2 = ((bf16[16,256,128]{2,1,0:T(8,128)(2,1)}), bf16[16,256,128]{2,1,0:T(8,128)(2,1)S(1)}, u32[]{:S(2)}, u32[]{:S(2)}) async-start(bf16[16,256,128]{2,1,0:T(8,128)(2,1)} %copy-done.5), calls=%async_computation.2 | async-start | bytes 2097152 | tf_op jit(solution)/shard_map/all_to_all | solution.py:266
  70.6 0.3 collective-permute-done.4.other_ref
  70.9 4.0 %scores.1 = bf16[256,8192]{1,0:T(8,128)(2,1)} custom-call(s32[3]{0:T(128)S(1)} %pad_add_fusion.at_ref, f32[256,256]{1,0:T(8,128)S(1)} %get-tuple-element.35.keep_ref, bf16[256,256]{1,0:T(8,128)(2,1)S(1)} %collective-permute-done.3.got_ref, bf16[16,512,128]{2,1,0:T(8,128)(2,1)S(1)} %all-to-all-done.1.own_ref, ...), custom_call_target="tpu_custom_call" | custom-call | flops 1073741824 | bytes 8388608 | tf_op jit(solution)/shard_map/scores/pallas_call | solution.py:234
  74.8 15.0 %all-to-all-done.2.in_ref = bf16[16,256,128]{2,1,0:T(8,128)(2,1)S(1)} async-done(((bf16[16,256,128]{2,1,0:T(8,128)(2,1)}), bf16[16,256,128]{2,1,0:T(8,128)(2,1)S(1)}, u32[]{:S(2)}, u32[]{:S(2)}) %all-to-all-start.2) | async-done | bytes 1048608 | tf_op jit(solution)/shard_map/all_to_all | solution.py:266
  89.8 0.2 fold.1
  90.0 2.3 %collective-permute-start.5 = (bf16[64,128]{1,0:T(8,128)(2,1)S(1)}, bf16[64,128]{1,0:T(8,128)(2,1)S(1)}, u32[]{:S(2)}, u32[]{:S(2)}) collective-permute-start(bf16[64,128]{1,0:T(8,128)(2,1)S(1)} %get-tuple-element.40), channel_id=1, source_target_pairs={{0,4},{1,5},{2,6},{3,7},{4,8},{5,9},{6,10},{7,11},{8,12},{9,13},{1... | collective-permute-start | bytes 49160 | tf_op jit(solution)/shard_map/ppermute | solution.py:271
  92.3 2.2 %collective-permute-start.7 = (bf16[64,128]{1,0:T(8,128)(2,1)S(1)}, bf16[64,128]{1,0:T(8,128)(2,1)S(1)}, u32[]{:S(2)}, u32[]{:S(2)}) collective-permute-start(bf16[64,128]{1,0:T(8,128)(2,1)S(1)} %get-tuple-element.42), channel_id=1, source_target_pairs={{0,12},{1,13},{2,14},{3,15},{4,0},{5,1},{6,2},{7,3},{8,4},{9,5},{1... | collective-permute-start | bytes 49160 | tf_op jit(solution)/shard_map/ppermute | solution.py:271
  94.5 1.6 %collective-permute-done.6 = bf16[64,128]{1,0:T(8,128)(2,1)S(1)} collective-permute-done((bf16[64,128]{1,0:T(8,128)(2,1)S(1)}, bf16[64,128]{1,0:T(8,128)(2,1)S(1)}, u32[]{:S(2)}, u32[]{:S(2)}) %collective-permute-start.6) | collective-permute-done | bytes 16416 | tf_op jit(solution)/shard_map/ppermute | solution.py:271
  96.1 0.6 div.10
  (16 shorter events, 0.3 us)
Async XLA Ops:
  0.6 1.6 %copy-start.2 = (bf16[4096,256]{1,0:T(8,128)(2,1)S(1)}, bf16[4096,256]{1,0:T(8,128)(2,1)}, u32[]{:S(2)}) copy-start(bf16[4096,256]{1,0:T(8,128)(2,1)} %factor_ref.3) | copy-start | bytes 6291460
  2.2 1.0 %copy-start.6 = (bf16[64,4096]{1,0:T(8,128)(2,1)S(1)}, bf16[64,4096]{1,0:T(8,128)(2,1)}, u32[]{:S(2)}) copy-start(bf16[64,4096]{1,0:T(8,128)(2,1)} %test_ref.1) | copy-start | bytes 1572868
  3.3 8.4 %copy-start.3 = (bf16[4096,256]{1,0:T(8,128)(2,1)S(1)}, bf16[4096,256]{1,0:T(8,128)(2,1)}, u32[]{:S(2)}) copy-start(bf16[4096,256]{1,0:T(8,128)(2,1)} %factor_ref.3) | copy-start | bytes 6291460
  3.8 11.9 %collective-permute-start = (bf16[64,256]{1,0:T(8,128)(2,1)S(1)}, bf16[64,256]{1,0:T(8,128)(2,1)S(1)}, u32[]{:S(2)}, u32[]{:S(2)}) collective-permute-start(bf16[64,256]{1,0:T(8,128)(2,1)S(1)} %get-tuple-element.24), channel_id=1, source_target_pairs={{0,1},{1,0},{2,3},{3,2},{4,5},{5,4},{6,7},{7,6},{8,9},{9,8},{10,11... | collective-permute-start | bytes 98312 | tf_op jit(solution)/shard_map/ppermute | solution.py:250
  11.7 2.2 %copy-start = (bf16[512,4096]{1,0:T(8,128)(2,1)S(1)}, bf16[512,4096]{1,0:T(8,128)(2,1)}, u32[]{:S(2)}) copy-start(bf16[512,4096]{1,0:T(8,128)(2,1)} %train_ref.3) | copy-start | bytes 12582916
  16.4 10.1 %all-to-all-start = ((bf16[8,64,128]{2,1,0:T(8,128)(2,1)}), bf16[8,64,128]{2,1,0:T(8,128)(2,1)S(1)}, u32[]{:S(2)}, u32[]{:S(2)}) async-start(bf16[8,64,128]{2,1,0:T(8,128)(2,1)} %sum_halves.1), calls=%async_computation | async-start | bytes 262144 | tf_op jit(solution)/shard_map/all_to_all | solution.py:253
  26.8 1.3 %copy-start.4 = (bf16[16,512,128]{2,1,0:T(8,128)(2,1)}, bf16[16,512,128]{2,1,0:T(8,128)(2,1)S(1)}, u32[]{:S(2)}) copy-start(bf16[16,512,128]{2,1,0:T(8,128)(2,1)S(1)} %spread.1) | copy-start | bytes 6291460
  28.1 36.4 %all-to-all-start.1 = ((bf16[16,512,128]{2,1,0:T(8,128)(2,1)}), bf16[16,512,128]{2,1,0:T(8,128)(2,1)S(1)}, u32[]{:S(2)}, u32[]{:S(2)}) async-start(bf16[16,512,128]{2,1,0:T(8,128)(2,1)} %copy-done.4), calls=%async_computation.1 | async-start | bytes 4194304 | tf_op jit(solution)/shard_map/all_to_all | solution.py:262
  34.8 9.7 %collective-permute-start.1 = (bf16[512,256]{1,0:T(8,128)(2,1)S(1)}, bf16[512,256]{1,0:T(8,128)(2,1)S(1)}, u32[]{:S(2)}, u32[]{:S(2)}) collective-permute-start(bf16[512,256]{1,0:T(8,128)(2,1)S(1)} %slice.3), channel_id=1, source_target_pairs={{0,1},{2,3},{4,5},{6,7},{8,9},{10,11},{12,13},{14,15},{16,17},{18,... | collective-permute-start | bytes 786440 | tf_op jit(solution)/shard_map/ppermute | solution.py:257
  44.5 2.2 %copy-start.1 = (bf16[512,4096]{1,0:T(8,128)(2,1)S(1)}, bf16[512,4096]{1,0:T(8,128)(2,1)}, u32[]{:S(2)}) copy-start(bf16[512,4096]{1,0:T(8,128)(2,1)} %train_ref.3) | copy-start | bytes 12582916
  48.6 8.5 %collective-permute-start.2 = (bf16[16,256,128]{2,1,0:T(8,128)(2,1)S(1)}, bf16[16,256,128]{2,1,0:T(8,128)(2,1)S(1)}, u32[]{:S(2)}, u32[]{:S(2)}) collective-permute-start(bf16[16,256,128]{2,1,0:T(8,128)(2,1)S(1)} %get-tuple-element.32), channel_id=1, source_target_pairs={{0,2},{1,3},{2,0},{3,1},{4,6},{5,7},{6,4},{7,5},{8,10},{9,11},{10,... | collective-permute-start | bytes 3145736 | tf_op jit(solution)/shard_map/ppermute | solution.py:261
  50.9 10.0 %collective-permute-start.3 = (bf16[256,256]{1,0:T(8,128)(2,1)S(1)}, bf16[256,256]{1,0:T(8,128)(2,1)S(1)}, u32[]{:S(2)}, u32[]{:S(2)}) collective-permute-start(bf16[256,256]{1,0:T(8,128)(2,1)S(1)} %get-tuple-element.33), channel_id=1, source_target_pairs={{0,1},{1,0},{2,3},{3,2},{4,5},{5,4},{6,7},{7,6},{8,9},{9,8},{10,11... | collective-permute-start | bytes 393224 | tf_op jit(solution)/shard_map/ppermute | solution.py:259
  57.3 1.0 %copy-start.5 = (bf16[16,256,128]{2,1,0:T(8,128)(2,1)}, bf16[16,256,128]{2,1,0:T(8,128)(2,1)S(1)}, u32[]{:S(2)}) copy-start(bf16[16,256,128]{2,1,0:T(8,128)(2,1)S(1)} %sum_cores.1) | copy-start | bytes 3145732
  64.5 6.3 %collective-permute-start.4 = (bf16[16,512,128]{2,1,0:T(8,128)(2,1)S(1)}, bf16[16,512,128]{2,1,0:T(8,128)(2,1)}, u32[]{:S(2)}, u32[]{:S(2)}) collective-permute-start(bf16[16,512,128]{2,1,0:T(8,128)(2,1)S(1)} %all-to-all-done.1.own_ref), channel_id=1, source_target_pairs={{0,2},{1,3},{2,0},{3,1},{4,6},{5,7},{6,4},{7,5},{8,10},{9,11},{10,... | collective-permute-start | bytes 6291464 | tf_op jit(solution)/shard_map/ppermute | solution.py:265
  66.9 22.9 %all-to-all-start.2 = ((bf16[16,256,128]{2,1,0:T(8,128)(2,1)}), bf16[16,256,128]{2,1,0:T(8,128)(2,1)S(1)}, u32[]{:S(2)}, u32[]{:S(2)}) async-start(bf16[16,256,128]{2,1,0:T(8,128)(2,1)} %copy-done.5), calls=%async_computation.2 | async-start | bytes 2097152 | tf_op jit(solution)/shard_map/all_to_all | solution.py:266
  90.0 4.5 %collective-permute-start.5 = (bf16[64,128]{1,0:T(8,128)(2,1)S(1)}, bf16[64,128]{1,0:T(8,128)(2,1)S(1)}, u32[]{:S(2)}, u32[]{:S(2)}) collective-permute-start(bf16[64,128]{1,0:T(8,128)(2,1)S(1)} %get-tuple-element.40), channel_id=1, source_target_pairs={{0,4},{1,5},{2,6},{3,7},{4,8},{5,9},{6,10},{7,11},{8,12},{9,13},{1... | collective-permute-start | bytes 49160 | tf_op jit(solution)/shard_map/ppermute | solution.py:271
  92.3 3.8 %collective-permute-start.6 = (bf16[64,128]{1,0:T(8,128)(2,1)S(1)}, bf16[64,128]{1,0:T(8,128)(2,1)S(1)}, u32[]{:S(2)}, u32[]{:S(2)}) collective-permute-start(bf16[64,128]{1,0:T(8,128)(2,1)S(1)} %get-tuple-element.41), channel_id=1, source_target_pairs={{0,8},{1,9},{2,10},{3,11},{4,12},{5,13},{6,14},{7,15},{8,0},{9,1},... | collective-permute-start | bytes 49160 | tf_op jit(solution)/shard_map/ppermute | solution.py:271
  92.3 3.8 %collective-permute-start.7 = (bf16[64,128]{1,0:T(8,128)(2,1)S(1)}, bf16[64,128]{1,0:T(8,128)(2,1)S(1)}, u32[]{:S(2)}, u32[]{:S(2)}) collective-permute-start(bf16[64,128]{1,0:T(8,128)(2,1)S(1)} %get-tuple-element.42), channel_id=1, source_target_pairs={{0,12},{1,13},{2,14},{3,15},{4,0},{5,1},{6,2},{7,3},{8,4},{9,5},{1... | collective-permute-start | bytes 49160 | tf_op jit(solution)/shard_map/ppermute | solution.py:271

commit v4 on v3

--- a/solution.py
+++ b/solution.py
@@ -251,16 +251,16 @@
     keep, give = train_parts(at, train_feats, factor_panel)
     parts, give = lax.optimization_barrier((parts, give))
     parts = lax.all_to_all(parts, ("l", "c"), 0, 0, tiled=True)
-    parts, first = lax.optimization_barrier((parts, train_feats[:, :W]))
     tests = spread(parts)
 
-    sent = lax.ppermute(first, AXES, TO_SECOND_HALF)
+    feats, _ = lax.optimization_barrier((train_feats, tests))
+    sent = lax.ppermute(feats[:, :W], AXES, TO_SECOND_HALF)
     sent, give, _ = lax.optimization_barrier((sent, give, tests))
     got = lax.ppermute(give, AXES, OTHER_HALF)
     mine, theirs = gram_terms(at, sent, train_feats)
     rows = sum_cores(mine, lax.ppermute(theirs, AXES, OTHER_CORE))
     tests = lax.all_to_all(tests, ("y", "x"), 0, 0, tiled=True)
-    tests, rows, got = lax.optimization_barrier((tests, rows, got))
+    tests, rows = lax.optimization_barrier((tests, rows))
 
     other = lax.ppermute(tests, AXES, OTHER_CORE)
     rows = lax.all_to_all(rows, ("y", "x"), 0, 0, tiled=True)

time: 98.3 us -> 95.8 us (0.975)
  blocking collectives: 0 us -> 9.76 us
  starting transfers between devices: 43.2 us -> 35.1 us
  waiting for transfers between devices: 32.2 us -> 29.1 us
    all_to_all x1, waiting for transfers between devices: 15 us -> 3.29 us  [local(): rows = lax.all_to_all(rows, ('y', 'x'), 0, 0, tiled=True)]
    all_to_all x0 -> x1, blocking collectives: none -> 9.76 us  [local(): parts = lax.all_to_all(parts, ('l', 'c'), 0, 0, tiled=True)]
    ppermute x1, waiting for transfers between devices: 2.58 us -> 8.43 us  [local(): got = lax.ppermute(give, AXES, OTHER_HALF)]
    all_to_all x1, waiting for transfers between devices: 3.61 us -> 9.18 us  [local(): tests = lax.all_to_all(tests, ('y', 'x'), 0, 0, tiled=True)]
    all_to_all x1 -> x0, waiting for transfers between devices: 4.87 us -> none  [local(): parts = lax.all_to_all(parts, ('l', 'c'), 0, 0, tiled=True)]
    all_to_all x1 -> x0, starting transfers between devices: 4.24 us -> none  [local(): parts = lax.all_to_all(parts, ('l', 'c'), 0, 0, tiled=True)]
    ppermute x1, starting transfers between devices: 6.23 us -> 3.5 us  [local(): got = lax.ppermute(give, AXES, OTHER_HALF)]
    ppermute x1, waiting for transfers between devices: 0.01 us -> 2.29 us  [local(): rows = sum_cores(mine, lax.ppermute(theirs, AXES, OTHER_CORE))]
  transfers between devices with their start and end apart: 11 -> 10, of which waited for: 7 -> 7; matrix products, arithmetic and copies ran while one was open for 1% -> 1% of each run, Pallas kernels for 8% -> 8%
where the time goes in v4:
time: 95.8 us; the launch traced here: 94.6 us
  starting transfers between devices  35.1 us (37%)
  waiting for transfers between devices  29.1 us (30%)
  local copies, waits for them, and re-layouts  10.9 us (11%)
  blocking collectives  9.76 us (10%)
  Pallas kernels  8.91 us (9%)
    all_to_all x1, blocking collectives, local(): parts = lax.all_to_all(parts, ('l', 'c'), 0, 0, tiled=True)  9.76 us
    unnamed x14, local copies, waits for them, and re-layouts  9.3 us
    all_to_all x1, waiting for transfers between devices, local(): tests = lax.all_to_all(tests, ('y', 'x'), 0, 0, tiled=True)  9.18 us
    ppermute x1, waiting for transfers between devices, local(): got = lax.ppermute(give, AXES, OTHER_HALF)  8.43 us
    ppermute x1, starting transfers between devices, local(): parts = sum_halves(test_keep, lax.ppermute(test_give, AXES, OTHER_HALF))  7.83 us
    all_to_all x1, starting transfers between devices, local(): tests = lax.all_to_all(tests, ('y', 'x'), 0, 0, tiled=True)  6.76 us
    ppermute x1, starting transfers between devices, local(): sent = lax.ppermute(feats[:, :W], AXES, TO_SECOND_HALF)  5.33 us
    ppermute x1, waiting for transfers between devices, local(): sent = lax.ppermute(feats[:, :W], AXES, TO_SECOND_HALF)  4.31 us
  transfers between devices with their start and end apart: 10, of which 7 were waited for; matrix products, arithmetic and copies ran while one was open for 1% of the time, Pallas kernels for 8%

profile of v4, /device:TPU:1, one launch (start us, length us, event | category | flops | bytes accessed | tf_op | source)
XLA Modules:
  0.0 94.6 jit_solution(2945032394448054792)
XLA Ops:
  0.6 1.6 %copy-done.2 = bf16[4096,256]{1,0:T(8,128)(2,1)S(1)} copy-done((bf16[4096,256]{1,0:T(8,128)(2,1)S(1)}, bf16[4096,256]{1,0:T(8,128)(2,1)}, u32[]{:S(2)}) %copy-start.2) | copy-done | bytes 2097176
  2.2 1.0 %copy-done.6 = bf16[64,4096]{1,0:T(8,128)(2,1)S(1)} copy-done((bf16[64,4096]{1,0:T(8,128)(2,1)S(1)}, bf16[64,4096]{1,0:T(8,128)(2,1)}, u32[]{:S(2)}) %copy-start.6) | copy-done | bytes 524312
  3.3 0.5 test_parts.1
  3.8 7.8 %collective-permute-start = (bf16[64,256]{1,0:T(8,128)(2,1)S(1)}, bf16[64,256]{1,0:T(8,128)(2,1)S(1)}, u32[]{:S(2)}, u32[]{:S(2)}) collective-permute-start(bf16[64,256]{1,0:T(8,128)(2,1)S(1)} %get-tuple-element.22), channel_id=1, source_target_pairs={{0,1},{1,0},{2,3},{3,2},{4,5},{5,4},{6,7},{7,6},{8,9},{9,8},{10,11... | collective-permute-start | bytes 98312 | tf_op jit(solution)/shard_map/ppermute | solution.py:250
  11.7 2.2 %copy-done = bf16[512,4096]{1,0:T(8,128)(2,1)S(1)} copy-done((bf16[512,4096]{1,0:T(8,128)(2,1)S(1)}, bf16[512,4096]{1,0:T(8,128)(2,1)}, u32[]{:S(2)}) %copy-start) | copy-done | bytes 4194328
  13.8 1.8 %train_parts.1 = (f32[256,256]{1,0:T(8,128)S(1)}, bf16[256,256]{1,0:T(8,128)(2,1)S(1)}) custom-call(s32[3]{0:T(128)S(1)} %pad_add_fusion.at_ref, bf16[512,4096]{1,0:T(8,128)(2,1)S(1)} %copy-done, bf16[4096,256]{1,0:T(8,128)(2,1)S(1)} %copy-done.3), custom_call_target="tpu_custom_call" | custom-call | flops 1073741824 | bytes 7340032 | tf_op jit(solution)/shard_map/train_parts/pallas_call | solution.py:188
  15.7 9.8 %all_to_all.15.parts_ref = bf16[8,64,128]{2,1,0:T(8,128)(2,1)S(1)} all-to-all(bf16[8,64,128]{2,1,0:T(8,128)(2,1)S(1)} %sum_halves.1), channel_id=1, replica_groups=mesh['y'=4,'x'=4,'l'=4,'c'=2,'h'=2] {'l','c'}, dimensions={0} | all-to-all | bytes 262144 | tf_op jit(solution)/shard_map/all_to_all | solution.py:253
  25.5 0.3 spread.1
  25.8 1.3 %copy-done.4 = bf16[16,512,128]{2,1,0:T(8,128)(2,1)} copy-done((bf16[16,512,128]{2,1,0:T(8,128)(2,1)}, bf16[16,512,128]{2,1,0:T(8,128)(2,1)S(1)}, u32[]{:S(2)}) %copy-start.4) | copy-done | bytes 2097176
  27.1 6.8 %all-to-all-start.1 = ((bf16[16,512,128]{2,1,0:T(8,128)(2,1)}), bf16[16,512,128]{2,1,0:T(8,128)(2,1)S(1)}, u32[]{:S(2)}, u32[]{:S(2)}) async-start(bf16[16,512,128]{2,1,0:T(8,128)(2,1)} %copy-done.4), calls=%async_computation.1 | async-start | bytes 4194304 | tf_op jit(solution)/shard_map/all_to_all | solution.py:262
  33.9 1.0 %slice.3 = bf16[512,256]{1,0:T(8,128)(2,1)S(1)} slice(bf16[512,4096]{1,0:T(8,128)(2,1)} %train_ref.3), slice={[0:512], [0:256]} | slice | bytes 524288 | tf_op jit(solution)/shard_map/slice | solution.py:257
  34.9 5.3 %collective-permute-start.1 = (bf16[512,256]{1,0:T(8,128)(2,1)S(1)}, bf16[512,256]{1,0:T(8,128)(2,1)S(1)}, u32[]{:S(2)}, u32[]{:S(2)}) collective-permute-start(bf16[512,256]{1,0:T(8,128)(2,1)S(1)} %slice.3), channel_id=1, source_target_pairs={{0,1},{2,3},{4,5},{6,7},{8,9},{10,11},{12,13},{14,15},{16,17},{18,... | collective-permute-start | bytes 786440 | tf_op jit(solution)/shard_map/ppermute | solution.py:257
  40.2 4.3 %collective-permute-done.1.got_ref = bf16[512,256]{1,0:T(8,128)(2,1)S(1)} collective-permute-done((bf16[512,256]{1,0:T(8,128)(2,1)S(1)}, bf16[512,256]{1,0:T(8,128)(2,1)S(1)}, u32[]{:S(2)}, u32[]{:S(2)}) %collective-permute-start.1) | collective-permute-done | bytes 262176 | tf_op jit(solution)/shard_map/ppermute | solution.py:257
  44.5 2.2 %copy-done.1 = bf16[512,4096]{1,0:T(8,128)(2,1)S(1)} copy-done((bf16[512,4096]{1,0:T(8,128)(2,1)S(1)}, bf16[512,4096]{1,0:T(8,128)(2,1)}, u32[]{:S(2)}) %copy-start.1) | copy-done | bytes 4194328
  46.7 1.9 %gram_terms.1 = (f32[16,256,128]{2,1,0:T(8,128)S(1)}, bf16[16,256,128]{2,1,0:T(8,128)(2,1)S(1)}) custom-call(s32[3]{0:T(128)S(1)} %pad_add_fusion.at_ref, bf16[512,256]{1,0:T(8,128)(2,1)S(1)} %collective-permute-done.1.got_ref, bf16[512,4096]{1,0:T(8,128)(2,1)S(1)} %copy-done.1), custom_call_target="tpu_custom_call" | custom-call | flops 1073741824 | bytes 7340032 | tf_op jit(solution)/shard_map/gram_terms/pallas_call | solution.py:87
  48.7 2.3 %collective-permute-start.2 = (bf16[16,256,128]{2,1,0:T(8,128)(2,1)S(1)}, bf16[16,256,128]{2,1,0:T(8,128)(2,1)S(1)}, u32[]{:S(2)}, u32[]{:S(2)}) collective-permute-start(bf16[16,256,128]{2,1,0:T(8,128)(2,1)S(1)} %get-tuple-element.29), channel_id=1, source_target_pairs={{0,2},{1,3},{2,0},{3,1},{4,6},{5,7},{6,4},{7,5},{8,10},{9,11},{10,... | collective-permute-start | bytes 3145736 | tf_op jit(solution)/shard_map/ppermute | solution.py:261
  50.9 2.3 %collective-permute-done.2.got_ref = bf16[16,256,128]{2,1,0:T(8,128)(2,1)S(1)} collective-permute-done((bf16[16,256,128]{2,1,0:T(8,128)(2,1)S(1)}, bf16[16,256,128]{2,1,0:T(8,128)(2,1)S(1)}, u32[]{:S(2)}, u32[]{:S(2)}) %collective-permute-start.2) | collective-permute-done | bytes 1048608 | tf_op jit(solution)/shard_map/ppermute | solution.py:261
  53.4 1.0 %copy-done.5 = bf16[16,256,128]{2,1,0:T(8,128)(2,1)} copy-done((bf16[16,256,128]{2,1,0:T(8,128)(2,1)}, bf16[16,256,128]{2,1,0:T(8,128)(2,1)S(1)}, u32[]{:S(2)}) %copy-start.5) | copy-done | bytes 1048600
  54.4 9.2 %all-to-all-done.1.own_ref = bf16[16,512,128]{2,1,0:T(8,128)(2,1)S(1)} async-done(((bf16[16,512,128]{2,1,0:T(8,128)(2,1)}), bf16[16,512,128]{2,1,0:T(8,128)(2,1)S(1)}, u32[]{:S(2)}, u32[]{:S(2)}) %all-to-all-start.1) | async-done | bytes 2097184 | tf_op jit(solution)/shard_map/all_to_all | solution.py:262
  63.6 2.4 %collective-permute-start.4 = (bf16[16,512,128]{2,1,0:T(8,128)(2,1)S(1)}, bf16[16,512,128]{2,1,0:T(8,128)(2,1)}, u32[]{:S(2)}, u32[]{:S(2)}) collective-permute-start(bf16[16,512,128]{2,1,0:T(8,128)(2,1)S(1)} %all-to-all-done.1.own_ref), channel_id=1, source_target_pairs={{0,2},{1,3},{2,0},{3,1},{4,6},{5,7},{6,4},{7,5},{8,10},{9,11},{10,... | collective-permute-start | bytes 6291464 | tf_op jit(solution)/shard_map/ppermute | solution.py:265
  66.0 3.7 %all-to-all-start.2 = ((bf16[16,256,128]{2,1,0:T(8,128)(2,1)}), bf16[16,256,128]{2,1,0:T(8,128)(2,1)S(1)}, u32[]{:S(2)}, u32[]{:S(2)}) async-start(bf16[16,256,128]{2,1,0:T(8,128)(2,1)} %copy-done.5), calls=%async_computation.2 | async-start | bytes 2097152 | tf_op jit(solution)/shard_map/all_to_all | solution.py:266
  69.6 3.5 %collective-permute-start.3 = (bf16[256,256]{1,0:T(8,128)(2,1)S(1)}, bf16[256,256]{1,0:T(8,128)(2,1)S(1)}, u32[]{:S(2)}, u32[]{:S(2)}) collective-permute-start(bf16[256,256]{1,0:T(8,128)(2,1)S(1)} %get-tuple-element.32), channel_id=1, source_target_pairs={{0,1},{1,0},{2,3},{3,2},{4,5},{5,4},{6,7},{7,6},{8,9},{9,8},{10,11... | collective-permute-start | bytes 393224 | tf_op jit(solution)/shard_map/ppermute | solution.py:259
  73.1 8.4 %collective-permute-done.3.got_ref = bf16[256,256]{1,0:T(8,128)(2,1)S(1)} collective-permute-done((bf16[256,256]{1,0:T(8,128)(2,1)S(1)}, bf16[256,256]{1,0:T(8,128)(2,1)S(1)}, u32[]{:S(2)}, u32[]{:S(2)}) %collective-permute-start.3) | collective-permute-done | bytes 131104 | tf_op jit(solution)/shard_map/ppermute | solution.py:259
  81.6 4.0 %scores.1 = bf16[256,8192]{1,0:T(8,128)(2,1)} custom-call(s32[3]{0:T(128)S(1)} %pad_add_fusion.at_ref, f32[256,256]{1,0:T(8,128)S(1)} %get-tuple-element.31.keep_ref, bf16[256,256]{1,0:T(8,128)(2,1)S(1)} %collective-permute-done.3.got_ref, bf16[16,512,128]{2,1,0:T(8,128)(2,1)S(1)} %all-to-all-done.1.own_ref, ...), custom_call_target="tpu_custom_call" | custom-call | flops 1073741824 | bytes 8388608 | tf_op jit(solution)/shard_map/scores/pallas_call | solution.py:234
  85.6 3.3 %all-to-all-done.2.in_ref = bf16[16,256,128]{2,1,0:T(8,128)(2,1)S(1)} async-done(((bf16[16,256,128]{2,1,0:T(8,128)(2,1)}), bf16[16,256,128]{2,1,0:T(8,128)(2,1)S(1)}, u32[]{:S(2)}, u32[]{:S(2)}) %all-to-all-start.2) | async-done | bytes 1048608 | tf_op jit(solution)/shard_map/all_to_all | solution.py:266
  88.9 0.2 fold.1
  89.0 1.0 %collective-permute-start.5 = (bf16[64,128]{1,0:T(8,128)(2,1)S(1)}, bf16[64,128]{1,0:T(8,128)(2,1)S(1)}, u32[]{:S(2)}, u32[]{:S(2)}) collective-permute-start(bf16[64,128]{1,0:T(8,128)(2,1)S(1)} %get-tuple-element.36), channel_id=1, source_target_pairs={{0,4},{1,5},{2,6},{3,7},{4,8},{5,9},{6,10},{7,11},{8,12},{9,13},{1... | collective-permute-start | bytes 49160 | tf_op jit(solution)/shard_map/ppermute | solution.py:271
  90.1 0.8 collective-permute-start.6
  90.8 1.5 %collective-permute-start.7 = (bf16[64,128]{1,0:T(8,128)(2,1)S(1)}, bf16[64,128]{1,0:T(8,128)(2,1)S(1)}, u32[]{:S(2)}, u32[]{:S(2)}) collective-permute-start(bf16[64,128]{1,0:T(8,128)(2,1)S(1)} %get-tuple-element.38), channel_id=1, source_target_pairs={{0,12},{1,13},{2,14},{3,15},{4,0},{5,1},{6,2},{7,3},{8,4},{9,5},{1... | collective-permute-start | bytes 49160 | tf_op jit(solution)/shard_map/ppermute | solution.py:271
  92.4 1.1 %collective-permute-done.5 = bf16[64,128]{1,0:T(8,128)(2,1)S(1)} collective-permute-done((bf16[64,128]{1,0:T(8,128)(2,1)S(1)}, bf16[64,128]{1,0:T(8,128)(2,1)S(1)}, u32[]{:S(2)}, u32[]{:S(2)}) %collective-permute-start.5) | collective-permute-done | bytes 16416 | tf_op jit(solution)/shard_map/ppermute | solution.py:271
  93.5 0.4 collective-permute-done.6
  94.0 0.6 div.10
  (15 shorter events, 0.3 us)
Async XLA Ops:
  0.6 1.6 %copy-start.2 = (bf16[4096,256]{1,0:T(8,128)(2,1)S(1)}, bf16[4096,256]{1,0:T(8,128)(2,1)}, u32[]{:S(2)}) copy-start(bf16[4096,256]{1,0:T(8,128)(2,1)} %factor_ref.3) | copy-start | bytes 6291460
  2.2 1.0 %copy-start.6 = (bf16[64,4096]{1,0:T(8,128)(2,1)S(1)}, bf16[64,4096]{1,0:T(8,128)(2,1)}, u32[]{:S(2)}) copy-start(bf16[64,4096]{1,0:T(8,128)(2,1)} %test_ref.1) | copy-start | bytes 1572868
  3.3 8.4 %copy-start.3 = (bf16[4096,256]{1,0:T(8,128)(2,1)S(1)}, bf16[4096,256]{1,0:T(8,128)(2,1)}, u32[]{:S(2)}) copy-start(bf16[4096,256]{1,0:T(8,128)(2,1)} %factor_ref.3) | copy-start | bytes 6291460
  3.8 11.9 %collective-permute-start = (bf16[64,256]{1,0:T(8,128)(2,1)S(1)}, bf16[64,256]{1,0:T(8,128)(2,1)S(1)}, u32[]{:S(2)}, u32[]{:S(2)}) collective-permute-start(bf16[64,256]{1,0:T(8,128)(2,1)S(1)} %get-tuple-element.22), channel_id=1, source_target_pairs={{0,1},{1,0},{2,3},{3,2},{4,5},{5,4},{6,7},{7,6},{8,9},{9,8},{10,11... | collective-permute-start | bytes 98312 | tf_op jit(solution)/shard_map/ppermute | solution.py:250
  11.7 2.2 %copy-start = (bf16[512,4096]{1,0:T(8,128)(2,1)S(1)}, bf16[512,4096]{1,0:T(8,128)(2,1)}, u32[]{:S(2)}) copy-start(bf16[512,4096]{1,0:T(8,128)(2,1)} %train_ref.3) | copy-start | bytes 12582916
  25.8 1.3 %copy-start.4 = (bf16[16,512,128]{2,1,0:T(8,128)(2,1)}, bf16[16,512,128]{2,1,0:T(8,128)(2,1)S(1)}, u32[]{:S(2)}) copy-start(bf16[16,512,128]{2,1,0:T(8,128)(2,1)S(1)} %spread.1) | copy-start | bytes 6291460
  27.1 36.4 %all-to-all-start.1 = ((bf16[16,512,128]{2,1,0:T(8,128)(2,1)}), bf16[16,512,128]{2,1,0:T(8,128)(2,1)S(1)}, u32[]{:S(2)}, u32[]{:S(2)}) async-start(bf16[16,512,128]{2,1,0:T(8,128)(2,1)} %copy-done.4), calls=%async_computation.1 | async-start | bytes 4194304 | tf_op jit(solution)/shard_map/all_to_all | solution.py:262
  34.9 9.7 %collective-permute-start.1 = (bf16[512,256]{1,0:T(8,128)(2,1)S(1)}, bf16[512,256]{1,0:T(8,128)(2,1)S(1)}, u32[]{:S(2)}, u32[]{:S(2)}) collective-permute-start(bf16[512,256]{1,0:T(8,128)(2,1)S(1)} %slice.3), channel_id=1, source_target_pairs={{0,1},{2,3},{4,5},{6,7},{8,9},{10,11},{12,13},{14,15},{16,17},{18,... | collective-permute-start | bytes 786440 | tf_op jit(solution)/shard_map/ppermute | solution.py:257
  44.5 2.2 %copy-start.1 = (bf16[512,4096]{1,0:T(8,128)(2,1)S(1)}, bf16[512,4096]{1,0:T(8,128)(2,1)}, u32[]{:S(2)}) copy-start(bf16[512,4096]{1,0:T(8,128)(2,1)} %train_ref.3) | copy-start | bytes 12582916
  48.7 4.6 %collective-permute-start.2 = (bf16[16,256,128]{2,1,0:T(8,128)(2,1)S(1)}, bf16[16,256,128]{2,1,0:T(8,128)(2,1)S(1)}, u32[]{:S(2)}, u32[]{:S(2)}) collective-permute-start(bf16[16,256,128]{2,1,0:T(8,128)(2,1)S(1)} %get-tuple-element.29), channel_id=1, source_target_pairs={{0,2},{1,3},{2,0},{3,1},{4,6},{5,7},{6,4},{7,5},{8,10},{9,11},{10,... | collective-permute-start | bytes 3145736 | tf_op jit(solution)/shard_map/ppermute | solution.py:261
  53.4 1.0 %copy-start.5 = (bf16[16,256,128]{2,1,0:T(8,128)(2,1)}, bf16[16,256,128]{2,1,0:T(8,128)(2,1)S(1)}, u32[]{:S(2)}) copy-start(bf16[16,256,128]{2,1,0:T(8,128)(2,1)S(1)} %sum_cores.1) | copy-start | bytes 3145732
  63.6 18.0 %collective-permute-start.4 = (bf16[16,512,128]{2,1,0:T(8,128)(2,1)S(1)}, bf16[16,512,128]{2,1,0:T(8,128)(2,1)}, u32[]{:S(2)}, u32[]{:S(2)}) collective-permute-start(bf16[16,512,128]{2,1,0:T(8,128)(2,1)S(1)} %all-to-all-done.1.own_ref), channel_id=1, source_target_pairs={{0,2},{1,3},{2,0},{3,1},{4,6},{5,7},{6,4},{7,5},{8,10},{9,11},{10,... | collective-permute-start | bytes 6291464 | tf_op jit(solution)/shard_map/ppermute | solution.py:265
  66.0 22.9 %all-to-all-start.2 = ((bf16[16,256,128]{2,1,0:T(8,128)(2,1)}), bf16[16,256,128]{2,1,0:T(8,128)(2,1)S(1)}, u32[]{:S(2)}, u32[]{:S(2)}) async-start(bf16[16,256,128]{2,1,0:T(8,128)(2,1)} %copy-done.5), calls=%async_computation.2 | async-start | bytes 2097152 | tf_op jit(solution)/shard_map/all_to_all | solution.py:266
  69.6 11.9 %collective-permute-start.3 = (bf16[256,256]{1,0:T(8,128)(2,1)S(1)}, bf16[256,256]{1,0:T(8,128)(2,1)S(1)}, u32[]{:S(2)}, u32[]{:S(2)}) collective-permute-start(bf16[256,256]{1,0:T(8,128)(2,1)S(1)} %get-tuple-element.32), channel_id=1, source_target_pairs={{0,1},{1,0},{2,3},{3,2},{4,5},{5,4},{6,7},{7,6},{8,9},{9,8},{10,11... | collective-permute-start | bytes 393224 | tf_op jit(solution)/shard_map/ppermute | solution.py:259
  89.0 4.5 %collective-permute-start.5 = (bf16[64,128]{1,0:T(8,128)(2,1)S(1)}, bf16[64,128]{1,0:T(8,128)(2,1)S(1)}, u32[]{:S(2)}, u32[]{:S(2)}) collective-permute-start(bf16[64,128]{1,0:T(8,128)(2,1)S(1)} %get-tuple-element.36), channel_id=1, source_target_pairs={{0,4},{1,5},{2,6},{3,7},{4,8},{5,9},{6,10},{7,11},{8,12},{9,13},{1... | collective-permute-start | bytes 49160 | tf_op jit(solution)/shard_map/ppermute | solution.py:271
  90.1 3.9 %collective-permute-start.6 = (bf16[64,128]{1,0:T(8,128)(2,1)S(1)}, bf16[64,128]{1,0:T(8,128)(2,1)S(1)}, u32[]{:S(2)}, u32[]{:S(2)}) collective-permute-start(bf16[64,128]{1,0:T(8,128)(2,1)S(1)} %get-tuple-element.37), channel_id=1, source_target_pairs={{0,8},{1,9},{2,10},{3,11},{4,12},{5,13},{6,14},{7,15},{8,0},{9,1},... | collective-permute-start | bytes 49160 | tf_op jit(solution)/shard_map/ppermute | solution.py:271
  90.8 3.1 %collective-permute-start.7 = (bf16[64,128]{1,0:T(8,128)(2,1)S(1)}, bf16[64,128]{1,0:T(8,128)(2,1)S(1)}, u32[]{:S(2)}, u32[]{:S(2)}) collective-permute-start(bf16[64,128]{1,0:T(8,128)(2,1)S(1)} %get-tuple-element.38), channel_id=1, source_target_pairs={{0,12},{1,13},{2,14},{3,15},{4,0},{5,1},{6,2},{7,3},{8,4},{9,5},{1... | collective-permute-start | bytes 49160 | tf_op jit(solution)/shard_map/ppermute | solution.py:271
